TPU v7x, 32 devices: a whole 2x2x4 slice. The times are simulated.
32 devices in a mesh: groups: 2 (over x), dp: 2 (over core), tensor: 8 (over z, y).
Axes of the slice: x: 2, y: 2, z: 4, core: 2. Of those that a mesh axis runs over, the one named last changes fastest.
Arguments:
- convolution_branch_input: bfloat16 [256, 3, 16384], P(('groups', 'dp'), None, 'tensor'), parts along dimension 0, may hold values from -6 to 6
- gate_branch_input: bfloat16 [256, 3, 16384], P(('groups', 'dp'), None, 'tensor'), parts along dimension 0, may hold values from -6 to 6
- convolution_state: bfloat16 [256, 3, 16384], P(('groups', 'dp'), None, 'tensor'), parts along dimension 0, may hold values from -6 to 6
- initial_hidden_state: float32 [256, 16, 16384], P(('groups', 'dp'), None, 'tensor'), parts along dimension 0, may hold values from -6 to 6
- stream_adapter_index: int32 [256], P(('groups', 'dp')), parts along dimension 0, may hold values from 0 to 31, as said below
- convolution_weight: float32 [4, 16384], P(None, 'tensor'), may hold values from -3 to 3
- convolution_bias: float32 [16384], P('tensor'), may hold values from -3 to 3
- input_coefficient_projection: bfloat16 [16384, 544], P('tensor'), may hold values from -0.046875 to 0.046875
- step_size_norm_gain: float32 [512], replicated, may hold values from 0.1 to 1.9
- step_size_projection: bfloat16 [512, 16384], P(None, 'tensor'), may hold values from -0.25 to 0.25
- step_size_bias: float32 [16384], P('tensor'), may hold values from -4 to -1
- negated_diagonal: float32 [16, 16384], P(None, 'tensor'), may hold values from 0.5 to 16
- channel_skip_gain: float32 [16384], P('tensor'), may hold values from 0.5 to 1.5
- output_projection: bfloat16 [16384, 8192], P('tensor'), may hold values from -0.0625 to 0.0625
- adapter_down_factor: bfloat16 [32, 16384, 64], P(('dp', 'tensor')), may hold values from -0.046875 to 0.046875
- adapter_up_factor: bfloat16 [32, 64, 8192], P(('dp', 'tensor')), may hold values from -0.75 to 0.75
Outputs:
- layer_out: bfloat16 [256, 3, 8192], P(('groups', 'dp'), None, 'tensor'), parts along dimension 0
- state_out: float32 [256, 16, 16384], P(('groups', 'dp'), None, 'tensor'), parts along dimension 0
There are 2 independent parts, one for each index of `groups`. A program takes and returns all parts, laid end to end along the dimension named above; an argument that names none is the same for every part. Nothing has to cross between parts.
Inputs may be any that keep to these rules, and one draw needn't show every extreme that they name: `stream_adapter_index`: adapter a is held by the device of index a // 2 over dp and tensor together (dp slowest). Among the streams of one dp shard at most 8 use adapters of one owner device, and in every shard some owner device has exactly 8 of them.
All inputs are finite; a program needn't handle non-finite values.
Results may differ from a plain program's by a relative error of at most 0.0063.
Values may be sent and summed in bfloat16 or wider, within the bound.
A program may use at most 192 MiB of HBM per device.

v0:
```python
import jax
import jax.numpy as jnp
from jax import lax
from jax.sharding import PartitionSpec as P


def body(
    convolution_branch_input,
    gate_branch_input,
    convolution_state,
    initial_hidden_state,
    stream_adapter_index,
    convolution_weight,
    convolution_bias,
    input_coefficient_projection,
    step_size_norm_gain,
    step_size_projection,
    step_size_bias,
    negated_diagonal,
    channel_skip_gain,
    output_projection,
    adapter_down_factor,
    adapter_up_factor,
):
    n_dp = lax.axis_size("dp")
    tensor_parts = lax.axis_size("tensor")
    owners = n_dp * tensor_parts
    streams, steps, channel_count = convolution_branch_input.shape
    dt_rank = step_size_norm_gain.shape[0]
    states = negated_diagonal.shape[0]
    kernel = convolution_weight.shape[0]
    width = output_projection.shape[1]
    slice_part = width // tensor_parts
    owner_share = adapter_down_factor.shape[0]
    rank_width = adapter_down_factor.shape[2]
    capacity = max(2, 2 * streams // owners)
    full = jnp.concatenate([convolution_state, convolution_branch_input], axis=1)
    state = initial_hidden_state
    gathered = []
    for step in range(steps):
        window = full[:, step : step + kernel].astype(jnp.float32)
        mixed = jnp.sum(window * convolution_weight[None], axis=1) + convolution_bias
        conv_out = jax.nn.silu(mixed)
        conv_low = conv_out.astype(jnp.bfloat16)
        partial_proj = jnp.dot(
            conv_low, input_coefficient_projection, preferred_element_type=jnp.float32
        )
        projected = lax.psum(partial_proj, "tensor")
        dt_raw = projected[:, :dt_rank]
        in_coef = projected[:, dt_rank : dt_rank + states]
        out_coef = projected[:, dt_rank + states :]
        factor = lax.rsqrt(jnp.mean(dt_raw * dt_raw, axis=1, keepdims=True) + 1e-06)
        dt_low = (dt_raw * factor * step_size_norm_gain).astype(jnp.bfloat16)
        step_size = jax.nn.softplus(
            jnp.dot(dt_low, step_size_projection, preferred_element_type=jnp.float32)
            + step_size_bias
        )
        decay = jnp.exp(-step_size[:, None, :] * negated_diagonal[None])
        state = decay * state + step_size[:, None, :] * in_coef[:, :, None] * conv_out[:, None, :]
        read = jnp.sum(state * out_coef[:, :, None], axis=1) + channel_skip_gain * conv_out
        gated = read * jax.nn.silu(gate_branch_input[:, step].astype(jnp.float32))
        gathered.append(gated.astype(jnp.bfloat16))
    inner_y = jnp.stack(gathered, axis=1)
    owner = stream_adapter_index // owner_share
    local = stream_adapter_index % owner_share
    position = jnp.arange(streams, dtype=jnp.int32)
    before = (owner[:, None] == owner[None, :]) & (position[None, :] < position[:, None])
    current_tally = jnp.sum(before.astype(jnp.int32), axis=1)
    slot = owner * capacity + current_tally
    match = jnp.arange(owners * capacity, dtype=jnp.int32)[:, None] == slot[None, :]
    dispatch = match.astype(jnp.bfloat16)
    slot_local = jnp.sum(jnp.where(match, local[None, :], 0), axis=1).reshape(owners, capacity)
    outgoing = jnp.dot(
        dispatch,
        inner_y.reshape(streams, steps * channel_count),
        preferred_element_type=jnp.float32,
    )
    outgoing = outgoing.astype(jnp.bfloat16).reshape(owners, capacity, steps, channel_count)
    down_factor = adapter_down_factor.reshape(owner_share, tensor_parts, channel_count, rank_width)
    rows = lax.all_to_all(outgoing, ("dp", "tensor"), split_axis=0, concat_axis=0, tiled=True)
    idents = lax.all_to_all(slot_local, ("dp", "tensor"), split_axis=0, concat_axis=0, tiled=True)
    count = rows.shape[1]
    rows = rows.reshape(n_dp, tensor_parts, count, steps, channel_count)
    which = idents.reshape(n_dp, tensor_parts, count)[:, 0]
    select = (which[..., None] == jnp.arange(owner_share, dtype=jnp.int32)).astype(jnp.float32)
    every = jnp.einsum("itksc,atcr->iksar", rows, down_factor, preferred_element_type=jnp.float32)
    coeffs = jnp.einsum("iksar,ika->iksr", every, select).astype(jnp.bfloat16)
    up_factor_split = adapter_up_factor.reshape(owner_share, rank_width, tensor_parts, slice_part)
    spread = jnp.einsum(
        "iksr,arjc->ijksac", coeffs, up_factor_split, preferred_element_type=jnp.float32
    )
    delta = jnp.einsum("ijksac,ika->ijksc", spread, select).astype(jnp.bfloat16)
    delta = delta.reshape(owners, count, steps, slice_part)
    back = lax.all_to_all(delta, ("dp", "tensor"), split_axis=0, concat_axis=0, tiled=True)
    flat_rows = inner_y.reshape(streams * steps, channel_count)
    partial_value = jnp.dot(flat_rows, output_projection, preferred_element_type=jnp.float32)
    total = lax.psum_scatter(
        partial_value.reshape(streams, steps, width), "tensor", scatter_dimension=2, tiled=True
    )
    carried = jnp.dot(
        dispatch.T,
        back.reshape(owners * capacity, steps * slice_part),
        preferred_element_type=jnp.float32,
    )
    layer_out = (total + carried.reshape(streams, steps, slice_part)).astype(jnp.bfloat16)
    return (layer_out, state)


def solution(mesh):
    placed = (
        P(("groups", "dp"), None, "tensor"),
        P(("groups", "dp"), None, "tensor"),
        P(("groups", "dp"), None, "tensor"),
        P(("groups", "dp"), None, "tensor"),
        P(("groups", "dp")),
        P(None, "tensor"),
        P("tensor"),
        P("tensor", None),
        P(),
        P(None, "tensor"),
        P("tensor"),
        P(None, "tensor"),
        P("tensor"),
        P("tensor", None),
        P(("dp", "tensor"), None, None),
        P(("dp", "tensor"), None, None),
    )
    return jax.shard_map(
        body,
        mesh=mesh,
        in_specs=placed,
        out_specs=(P(("groups", "dp"), None, "tensor"), P(("groups", "dp"), None, "tensor")),
        check_vma=False,
    )
```

profile of v0, /device:TPU:9, one launch (start us, length us, event | category | flops | bytes accessed | tf_op | source)
XLA Modules:
  0.0 298.1 jit_solution(9812127069590118845)
XLA Ops:
  7.2 1.3 constant_dynamic-update-slice_fusion.1
  8.6 1.2 constant_dynamic-update-slice_fusion
  11.0 1.5 fusion.34
  12.5 1.5 fusion.36
  14.0 1.5 fusion.38
  15.5 71.7 %all-reduce.3.cloned.1.call-done = (f32[64,544]{1,0:T(8,128)}, f32[64,544]{1,0:T(8,128)}, f32[64,544]{1,0:T(8,128)}) async-done(((f32[64,544]{1,0:T(8,128)}, f32[64,544]{1,0:T(8,128)}, f32[64,544]{1,0:T(8,128)}), (f32[64,544]{1,0:T(8,128)}, f32[64,544]{1,0:T(8,128)}, f32[64,544]{1,0:T(8,128)})) %all-reduce.3.cloned.1.call-update) | async-done | bytes 417808 | tf_op jit(solution)/shard_map/psum | solution.py:48
  87.3 1.1 multiply_reduce_fusion.8
  88.3 0.9 fusion.60
  89.3 1.1 multiply_reduce_fusion.6
  90.4 0.9 fusion.62
  91.3 2.4 fusion.65
  93.7 0.7 fusion.64
  94.6 0.7 fusion.63
  95.8 15.2 %multiply_reduce_fusion.2 = (f32[64,2048]{1,0:T(8,128)S(1)}, f32[64,2048]{1,0:T(8,128)S(1)}, f32[64,2048]{1,0:T(8,128)S(1)}, f32[64,16,2048]{2,1,0:T(8,128)}) fusion(f32[64,16,2048]{2,1,0:T(8,128)} %param.19, f32[64,16]{1,0:T(8,128)S(1)} %get-tuple-element.39, f32[64,2048]{1,0:T(8,128)S(1)} %copy-done.6, f32[64,16]{1,0:T(8,128)S(1)} %get-tuple-element.38, ...), kind=kLoop, calls=%fused_computation.6 | loop fusion | flops 43646976 | bytes 23224320 | tf_op jit(solution)/shard_map/reduce_sum | solution.py:60
  111.0 0.8 fusion.32
  112.7 16.5 %fusion = f32[64,3,8192]{2,0,1:T(8,128)} fusion(bf16[2048,8192]{1,0:T(8,128)(2,1)} %param.29, bf16[64,1,2048]{2,0,1:T(8,128)(2,1)S(1)} %get-tuple-element.15, bf16[64,1,2048]{2,0,1:T(8,128)(2,1)S(1)} %get-tuple-element.16, bf16[64,1,2048]{2,0,1:T(8,128)(2,1)S(1)} %get-tuple-element.14), kind=kOutput, calls=%fused_computation | convolution fusion | flops 6443237376 | bytes 40632320 | tf_op jit(solution)/shard_map/dot_general | solution.py:96
  130.8 6.8 %all-to-all-start = ((s32[16,1,8]{2,1,0:T(1,128)}), s32[16,1,8]{2,1,0:T(1,128)S(1)}, u32[]{:S(2)}, u32[]{:S(2)}) async-start(s32[16,1,8]{2,1,0:T(1,128)} %bitcast.8), calls=%async_computation.1 | async-start | bytes 16384 | tf_op jit(solution)/shard_map/all_to_all | solution.py:81
  137.8 1.9 convolution_convert_fusion
  139.6 2.7 all-to-all-done
  142.4 6.0 %all-to-all-start.1 = ((bf16[16,8,3,2048]{3,1,2,0:T(8,128)(2,1)}), bf16[16,8,3,2048]{3,1,2,0:T(8,128)(2,1)}, u32[]{:S(2)}, u32[]{:S(2)}) async-start(bf16[16,8,3,2048]{3,1,2,0:T(8,128)(2,1)} %bitcast.12), calls=%async_computation.2 | async-start | bytes 3145728 | tf_op jit(solution)/shard_map/all_to_all | solution.py:80
  148.4 7.6 %copy.68 = bf16[16,8,8,2048]{3,2,1,0:T(8,128)(2,1)} copy(bf16[16,8,8,2048]{3,1,2,0:T(8,128)(2,1)} %bitcast.108) | data formatting | bytes 8388608
  155.9 1.4 copy.69
  157.4 1.5 bitcast_bitcast_fusion
  158.9 63.7 %all-to-all-done.1 = bf16[16,8,3,2048]{3,1,2,0:T(8,128)(2,1)} async-done(((bf16[16,8,3,2048]{3,1,2,0:T(8,128)(2,1)}), bf16[16,8,3,2048]{3,1,2,0:T(8,128)(2,1)}, u32[]{:S(2)}, u32[]{:S(2)}) %all-to-all-start.1) | async-done | bytes 1572896 | tf_op jit(solution)/shard_map/all_to_all | solution.py:80
  222.7 7.5 %fusion.13 = bf16[2,8,3,2,64]{4,1,3,2,0:T(8,128)(2,1)S(1)} fusion(bf16[2,8,2048,64,1,1]{2,1,3,0,5,4:T(8,128)(2,1)} %bitcast.109, bf16[2,8,8,3,2048,1]{4,2,3,1,0,5:T(8,128)(2,1)} %bitcast.14), kind=kOutput, calls=%fused_computation.30 | convolution fusion | flops 201326592 | bytes 5779456 | tf_op jit(solution)/shard_map/itksc,atcr->iksar/dot_general | solution.py:86
  230.3 2.7 fusion.8
  233.0 2.8 fusion.4
  235.8 0.8 copy.95
  236.7 23.6 %all_to_all.19 = bf16[16,8,3,1024]{3,1,2,0:T(8,128)(2,1)} all-to-all(bf16[16,8,3,1024]{3,1,2,0:T(8,128)(2,1)S(1)} %bitcast.113), channel_id=1, replica_groups=mesh['groups'=2,'dp'=2,'tensor'=8] {'dp','tensor'}, dimensions={0} | all-to-all | bytes 1572864 | tf_op jit(solution)/shard_map/all_to_all | solution.py:94
  260.2 1.6 copy.46
  261.8 27.1 %reduce-scatter.2.cloned.1.call-done = f32[64,3,1024]{2,0,1:T(8,128)} async-done(((f32[64,3,8192]{2,0,1:T(8,128)}), f32[64,3,1024]{2,0,1:T(8,128)}) %reduce-scatter.2.cloned.1.call-update) | async-done | bytes 786448 | tf_op jit(solution)/shard_map/reduce_scatter | solution.py:97
  288.9 2.3 fusion.12
  (73 shorter events, 4.7 us)
Async XLA Ops:
  7.2 3.8 %copy-start = (bf16[2048,544]{0,1:T(8,128)(2,1)S(1)}, bf16[2048,544]{0,1:T(8,128)(2,1)}, u32[]{:S(2)}) copy-start(bf16[2048,544]{0,1:T(8,128)(2,1)} %param.23) | copy-start | bytes 6684676
  7.2 2.6 copy-start.22
  7.2 80.1 %all-reduce.3.cloned.1.call-start = ((), (), s32[]{:S(2)}) async-start(), calls=%async_computation.5 | async-start | bytes 983040 | tf_op jit(solution)/shard_map/psum | solution.py:48
  9.8 0.7 copy-start.23
  10.3 2.1 copy-start.3
  10.9 3.0 %copy-start.7 = (f32[64,2048]{1,0:T(8,128)}, f32[64,2048]{1,0:T(8,128)S(1)}, u32[]{:S(2)}) copy-start(f32[64,2048]{1,0:T(8,128)S(1)} %get-tuple-element.24) | copy-start | bytes 1572868
  10.9 3.0 %copy-start.9 = (f32[64,2048]{1,0:T(8,128)}, f32[64,2048]{1,0:T(8,128)S(1)}, u32[]{:S(2)}) copy-start(f32[64,2048]{1,0:T(8,128)S(1)} %get-tuple-element.25) | copy-start | bytes 1572868
  10.9 3.0 %copy-start.5 = (f32[64,2048]{1,0:T(8,128)}, f32[64,2048]{1,0:T(8,128)S(1)}, u32[]{:S(2)}) copy-start(f32[64,2048]{1,0:T(8,128)S(1)} %get-tuple-element.23) | copy-start | bytes 1572868
  13.9 77.3 %copy-start.21 = (f32[2048]{0:T(1024)S(1)}, f32[2048]{0:T(1024)}, u32[]{:S(2)}) copy-start(f32[2048]{0:T(1024)} %param.26) | copy-start | bytes 24580
  13.9 77.4 %copy-start.24 = (f32[512]{0:T(512)S(1)}, f32[512]{0:T(512)}, u32[]{:S(2)}) copy-start(f32[512]{0:T(512)} %param.24) | copy-start | bytes 6148
  15.5 78.2 %copy-start.2 = (bf16[512,2048]{1,0:T(8,128)(2,1)S(1)}, bf16[512,2048]{1,0:T(8,128)(2,1)}, u32[]{:S(2)}) copy-start(bf16[512,2048]{1,0:T(8,128)(2,1)} %param.25) | copy-start | bytes 6291460
  15.5 273.4 %reduce-scatter.2.cloned.1.call-start = ((), (), s32[]{:S(2)}) async-start(), calls=%async_computation.4 | async-start | bytes 7077888 | tf_op jit(solution)/shard_map/reduce_scatter | solution.py:97
  87.3 6.4 %copy-start.19 = (f32[64,544]{1,0:T(8,128)S(1)}, f32[64,544]{1,0:T(8,128)}, u32[]{:S(2)}) copy-start(f32[64,544]{1,0:T(8,128)} %get-tuple-element.8) | copy-start | bytes 417796
  93.7 0.9 copy-start.18
  94.4 1.1 copy-start.6
  94.5 1.2 copy-start.8
  94.5 1.4 copy-start.10
  94.5 1.4 copy-start.20
  95.8 15.2 %copy-start.4 = (f32[64,2048]{1,0:T(8,128)S(1)}, f32[64,2048]{1,0:T(8,128)}, u32[]{:S(2)}) copy-start(f32[64,2048]{1,0:T(8,128)} %copy-done.3) | copy-start | bytes 1572868
  95.8 15.2 %copy-start.17 = (bf16[64,3,2048]{2,0,1:T(8,128)(2,1)S(1)}, bf16[64,3,2048]{2,0,1:T(8,128)(2,1)}, u32[]{:S(2)}) copy-start(bf16[64,3,2048]{2,0,1:T(8,128)(2,1)} %param.17) | copy-start | bytes 2359300
  95.8 15.2 %copy-start.25 = (f32[2048]{0:T(1024)S(1)}, f32[2048]{0:T(1024)}, u32[]{:S(2)}) copy-start(f32[2048]{0:T(1024)} %param.28) | copy-start | bytes 24580
  111.9 0.7 copy-start.13
  111.9 0.8 copy-start.15
  129.1 0.7 copy-start.26
  129.1 8.5 %copy-start.14 = (bf16[64,1,2048]{2,0,1:T(8,128)(2,1)S(1)}, bf16[64,1,2048]{2,0,1:T(8,128)(2,1)}, u32[]{:S(2)}) copy-start(bf16[64,1,2048]{2,0,1:T(8,128)(2,1)} %copy-done.13) | copy-start | bytes 786436
  129.1 8.5 %copy-start.16 = (bf16[64,1,2048]{2,0,1:T(8,128)(2,1)S(1)}, bf16[64,1,2048]{2,0,1:T(8,128)(2,1)}, u32[]{:S(2)}) copy-start(bf16[64,1,2048]{2,0,1:T(8,128)(2,1)} %copy-done.15) | copy-start | bytes 786436
  130.8 11.6 %all-to-all-start = ((s32[16,1,8]{2,1,0:T(1,128)}), s32[16,1,8]{2,1,0:T(1,128)S(1)}, u32[]{:S(2)}, u32[]{:S(2)}) async-start(s32[16,1,8]{2,1,0:T(1,128)} %bitcast.8), calls=%async_computation.1 | async-start | bytes 16384 | tf_op jit(solution)/shard_map/all_to_all | solution.py:81
  142.4 80.3 %all-to-all-start.1 = ((bf16[16,8,3,2048]{3,1,2,0:T(8,128)(2,1)}), bf16[16,8,3,2048]{3,1,2,0:T(8,128)(2,1)}, u32[]{:S(2)}, u32[]{:S(2)}) async-start(bf16[16,8,3,2048]{3,1,2,0:T(8,128)(2,1)} %bitcast.12), calls=%async_computation.2 | async-start | bytes 3145728 | tf_op jit(solution)/shard_map/all_to_all | solution.py:80
  148.3 7.6 %copy-start.11 = (bf16[2,64,8192]{2,1,0:T(8,128)(2,1)S(1)}, bf16[2,64,8192]{2,1,0:T(8,128)(2,1)}, u32[]{:S(2)}) copy-start(bf16[2,64,8192]{2,1,0:T(8,128)(2,1)} %param.31) | copy-start | bytes 6291460
  222.7 7.7 %copy-start.12 = (bf16[2,64,8,1024,1,1]{3,2,1,0,5,4:T(8,128)(2,1)S(1)}, bf16[2,64,8,1024,1,1]{3,2,1,0,5,4:T(8,128)(2,1)}, u32[]{:S(2)}) copy-start(bf16[2,64,8,1024,1,1]{3,2,1,0,5,4:T(8,128)(2,1)} %bitcast_bitcast_fusion) | copy-start | bytes 6291460
  236.6 54.6 %copy-start.1 = (bf16[2048,544]{0,1:T(8,128)(2,1)S(1)}, bf16[2048,544]{0,1:T(8,128)(2,1)}, u32[]{:S(2)}) copy-start(bf16[2048,544]{0,1:T(8,128)(2,1)} %param.23) | copy-start | bytes 6684676
Sparse Core Ops, SparseCore 0:
  15.6 71.6 all-reduce.2
  129.3 159.5 reduce-scatter.1
where the time goes:
time: 301 us; the launch traced here: 298 us
  waiting for transfers between devices  165 us (55%)
  matrix products  42 us (14%)
  blocking collectives  23.6 us (8%)
  local copies, waits for them, and re-layouts  20.3 us (7%)
  other arithmetic  19.6 us (7%)
  between operations  14.4 us (5%)
  starting transfers between devices  12.9 us (4%)
    psum x1, waiting for transfers between devices, body(): projected = lax.psum(partial_proj, 'tensor')  71.7 us
    all_to_all x1, waiting for transfers between devices, body(): lax.all_to_all(outgoing, ('dp', 'tensor'), split_axis=0, concat_axis=0, t...  63.7 us
    reduce_scatter x1, waiting for transfers between devices, body(): lax.psum_scatter(partial_value.reshape(streams, steps, width), 'tensor',...  27.1 us
    all_to_all x1, blocking collectives, body(): lax.all_to_all(delta, ('dp', 'tensor'), split_axis=0, concat_axis=0, tile...  23.6 us
    dot_general x1, matrix products, body(): jnp.dot(flat_rows, output_projection, preferred_element_type=jnp.float32)  16.5 us
    reduce_sum x1, other arithmetic, body(): jnp.sum(state * out_coef[:, :, None], axis=1) + channel_skip_gain * conv_out  15.2 us
    unnamed x57, local copies, waits for them, and re-layouts  12.6 us
    dot_general x1, matrix products, body(): jnp.einsum('itksc,atcr->iksar', rows, down_factor, preferred_element_type...  7.47 us
  transfers between devices with their start and end apart: 4, of which 4 were waited for; matrix products, arithmetic and copies ran while one was open for 10% of the time, Pallas kernels for 0%

commit v1 on v0

--- a/solution.py
+++ b/solution.py
@@ -1,7 +1,199 @@
+import functools
+
 import jax
 import jax.numpy as jnp
 from jax import lax
+from jax.experimental import pallas as pl
+from jax.experimental.pallas import tpu as pltpu
 from jax.sharding import PartitionSpec as P
+
+MESH = pl.DeviceIdType.MESH
+
+
+def norm_kernel(parts, dt_rank, part_ref, gain_ref, dt_ref, coef_ref, held, send_sem, recv_sem, send2, recv2, send3, recv3):
+    me = lax.axis_index("tensor")
+    barrier = pltpu.get_barrier_semaphore()
+    for k in range(1, parts):
+        peer = lax.rem(me + k, parts)
+        pl.semaphore_signal(barrier, inc=1, device_id={"tensor": peer}, device_id_type=MESH)
+    pl.semaphore_wait(barrier, parts - 1)
+    copies = []
+    for k in range(1, parts):
+        peer = lax.rem(me + k, parts)
+        copy = pltpu.make_async_remote_copy(
+            src_ref=part_ref.at[peer],
+            dst_ref=held.at[k - 1],
+            send_sem=send_sem.at[k - 1],
+            recv_sem=recv_sem.at[k - 1],
+            device_id={"tensor": peer},
+            device_id_type=MESH,
+        )
+        copy.start()
+        copies.append(copy)
+    total = part_ref[me]
+    for k in range(1, parts):
+        copies[k - 1].wait_recv()
+        total = total + held[k - 1]
+    dt_raw = total[:, :dt_rank]
+    factor = lax.rsqrt(jnp.mean(dt_raw * dt_raw, axis=1, keepdims=True) + 1e-06)
+    dt_low = dt_raw * factor * gain_ref[...]
+    rows = dt_low.shape[0]
+    padded = dt_ref.shape[1]
+    if padded > rows:
+        dt_low = jnp.concatenate([dt_low, jnp.zeros((padded - rows, dt_rank), jnp.float32)], axis=0)
+    dt_ref[me] = dt_low.astype(jnp.bfloat16)
+    coef_ref[me] = total[:, dt_rank:]
+    later = []
+    for k in range(1, parts):
+        peer = lax.rem(me + k, parts)
+        for ref, out_sem, in_sem in ((dt_ref, send2, recv2), (coef_ref, send3, recv3)):
+            copy = pltpu.make_async_remote_copy(
+                src_ref=ref.at[me],
+                dst_ref=ref.at[me],
+                send_sem=out_sem.at[k - 1],
+                recv_sem=in_sem.at[k - 1],
+                device_id={"tensor": peer},
+                device_id_type=MESH,
+            )
+            copy.start()
+            later.append(copy)
+    for copy in copies:
+        copy.wait_send()
+    for copy in later:
+        copy.wait()
+
+
+def summed_and_normed(partial, gain, parts, dt_rank):
+    rows, columns = partial.shape
+    share = rows // parts
+    padded = -(-share // 16) * 16
+    dma = pltpu.SemaphoreType.DMA((parts - 1,))
+    dt, coef = pl.pallas_call(
+        functools.partial(norm_kernel, parts, dt_rank),
+        out_shape=(
+            jax.ShapeDtypeStruct((parts, padded, dt_rank), jnp.bfloat16),
+            jax.ShapeDtypeStruct((parts, share, columns - dt_rank), jnp.float32),
+        ),
+        in_specs=[pl.BlockSpec(memory_space=pltpu.VMEM)] * 2,
+        out_specs=(pl.BlockSpec(memory_space=pltpu.VMEM),) * 2,
+        scratch_shapes=[
+            pltpu.VMEM((parts - 1, share, columns), jnp.float32),
+        ]
+        + [dma] * 6,
+        compiler_params=pltpu.CompilerParams(
+            collective_id=0, has_side_effects=True, vmem_limit_bytes=24 << 20
+        ),
+    )(partial.reshape(parts, share, columns), gain.reshape(1, dt_rank))
+    return dt[:, :share].reshape(rows, dt_rank), coef.reshape(rows, columns - dt_rank)
+
+
+def scatter_kernel(x_ref, out_ref, r0, r1, r2, a1, a2, send_sem, recv_sem):
+    me = lax.axis_index("tensor")
+    y, z = lax.rem(me, 2), me // 2
+    h = z // 2
+    c = lax.rem(z + h, 2)
+    bits = (y, c, h)
+
+    def place(sel):
+        far = sel[1] + sel[2] * (3 - 2 * sel[1])
+        return far * 2 + sel[0]
+
+    def flipped(d):
+        return tuple(1 - b if i == d else b for i, b in enumerate(bits))
+
+    barrier = pltpu.get_barrier_semaphore()
+    for d in range(3):
+        pl.semaphore_signal(barrier, inc=1, device_id={"tensor": place(flipped(d))}, device_id_type=MESH)
+    pl.semaphore_wait(barrier, 3)
+    width = out_ref.shape[1]
+    half = width // 2
+    orders = ((0, 1, 2), (1, 2, 0))
+
+    def send(flow, n, src, dst, d):
+        copy = pltpu.make_async_remote_copy(
+            src_ref=src,
+            dst_ref=dst,
+            send_sem=send_sem.at[flow * 7 + n],
+            recv_sem=recv_sem.at[flow * 7 + n],
+            device_id={"tensor": place(flipped(d))},
+            device_id_type=MESH,
+        )
+        copy.start()
+        return copy
+
+    def columns(flow, sel):
+        return pl.ds(pl.multiple_of(place(sel) * width + flow * half, 128), half)
+
+    def chosen(order, values):
+        sel = [None] * 3
+        for d, v in zip(order, values):
+            sel[d] = v
+        return tuple(sel)
+
+    first, second, third = [[], []], [[], []], [None, None]
+    for p in range(2):
+        for q in range(2):
+            for flow in range(2):
+                o = orders[flow]
+                b1 = 1 - bits[o[1]] if p == 0 else bits[o[1]]
+                sel = chosen(o, (1 - bits[o[0]], b1, q))
+                first[flow].append(send(flow, p * 2 + q, x_ref.at[:, columns(flow, sel)], r0.at[flow, p * 2 + q], o[0]))
+    for q in range(2):
+        for flow in range(2):
+            o = orders[flow]
+            first[flow][q].wait_recv()
+            sel = chosen(o, (bits[o[0]], 1 - bits[o[1]], q))
+            own = x_ref[:, columns(flow, sel)].astype(jnp.float32)
+            a1[flow, q] = (own + r0[flow, q].astype(jnp.float32)).astype(jnp.bfloat16)
+            second[flow].append(send(flow, 4 + q, a1.at[flow, q], r1.at[flow, q], o[1]))
+    for q in range(2):
+        for flow in range(2):
+            o = orders[flow]
+            first[flow][2 + q].wait_recv()
+            sel = chosen(o, (bits[o[0]], bits[o[1]], q))
+            own = x_ref[:, columns(flow, sel)].astype(jnp.float32)
+            a2[flow, q] = own + r0[flow, 2 + q].astype(jnp.float32)
+    for flow in range(2):
+        o = orders[flow]
+        for q in range(2):
+            second[flow][q].wait_recv()
+        want = 1 - bits[o[2]]
+        a1[flow, 2] = (a2[flow, want] + r1[flow, want].astype(jnp.float32)).astype(jnp.bfloat16)
+        third[flow] = send(flow, 6, a1.at[flow, 2], r2.at[flow], o[2])
+    for flow in range(2):
+        o = orders[flow]
+        keep = bits[o[2]]
+        third[flow].wait_recv()
+        out_ref[:, flow * half : (flow + 1) * half] = (
+            a2[flow, keep] + r1[flow, keep].astype(jnp.float32) + r2[flow].astype(jnp.float32)
+        ).astype(jnp.bfloat16)
+    for flow in range(2):
+        for copy in first[flow] + second[flow] + [third[flow]]:
+            copy.wait_send()
+
+
+def scattered(partial, parts):
+    rows, width = partial.shape
+    own = width // parts
+    half = own // 2
+    return pl.pallas_call(
+        scatter_kernel,
+        out_shape=jax.ShapeDtypeStruct((rows, own), jnp.bfloat16),
+        in_specs=[pl.BlockSpec(memory_space=pltpu.VMEM)],
+        out_specs=pl.BlockSpec(memory_space=pltpu.VMEM),
+        scratch_shapes=[
+            pltpu.VMEM((2, 4, rows, half), jnp.bfloat16),
+            pltpu.VMEM((2, 2, rows, half), jnp.bfloat16),
+            pltpu.VMEM((2, rows, half), jnp.bfloat16),
+            pltpu.VMEM((2, 3, rows, half), jnp.bfloat16),
+            pltpu.VMEM((2, 2, rows, half), jnp.float32),
+            pltpu.SemaphoreType.DMA((14,)),
+            pltpu.SemaphoreType.DMA((14,)),
+        ],
+        compiler_params=pltpu.CompilerParams(
+            collective_id=1, has_side_effects=True, vmem_limit_bytes=32 << 20
+        ),
+    )(partial)
 
 
 def body(
@@ -37,20 +229,32 @@
     full = jnp.concatenate([convolution_state, convolution_branch_input], axis=1)
     state = initial_hidden_state
     gathered = []
+    conv_outs = []
     for step in range(steps):
         window = full[:, step : step + kernel].astype(jnp.float32)
         mixed = jnp.sum(window * convolution_weight[None], axis=1) + convolution_bias
-        conv_out = jax.nn.silu(mixed)
-        conv_low = conv_out.astype(jnp.bfloat16)
-        partial_proj = jnp.dot(
-            conv_low, input_coefficient_projection, preferred_element_type=jnp.float32
-        )
+        conv_outs.append(jax.nn.silu(mixed))
+    conv_low = jnp.concatenate(conv_outs, axis=0).astype(jnp.bfloat16)
+    partial_proj = jnp.dot(
+        conv_low, input_coefficient_projection, preferred_element_type=jnp.float32
+    )
+    small = tensor_parts == 8 and n_dp == 2
+    if small:
+        dt_all, coef_all = summed_and_normed(
+            partial_proj, step_size_norm_gain, tensor_parts, dt_rank
+        )
+    else:
         projected = lax.psum(partial_proj, "tensor")
         dt_raw = projected[:, :dt_rank]
-        in_coef = projected[:, dt_rank : dt_rank + states]
-        out_coef = projected[:, dt_rank + states :]
         factor = lax.rsqrt(jnp.mean(dt_raw * dt_raw, axis=1, keepdims=True) + 1e-06)
-        dt_low = (dt_raw * factor * step_size_norm_gain).astype(jnp.bfloat16)
+        dt_all = (dt_raw * factor * step_size_norm_gain).astype(jnp.bfloat16)
+        coef_all = projected[:, dt_rank:]
+    for step in range(steps):
+        conv_out = conv_outs[step]
+        dt_low = dt_all[step * streams : (step + 1) * streams]
+        coef = coef_all[step * streams : (step + 1) * streams]
+        in_coef = coef[:, :states]
+        out_coef = coef[:, states:]
         step_size = jax.nn.softplus(
             jnp.dot(dt_low, step_size_projection, preferred_element_type=jnp.float32)
             + step_size_bias
@@ -85,24 +289,45 @@
     select = (which[..., None] == jnp.arange(owner_share, dtype=jnp.int32)).astype(jnp.float32)
     every = jnp.einsum("itksc,atcr->iksar", rows, down_factor, preferred_element_type=jnp.float32)
     coeffs = jnp.einsum("iksar,ika->iksr", every, select).astype(jnp.bfloat16)
-    up_factor_split = adapter_up_factor.reshape(owner_share, rank_width, tensor_parts, slice_part)
-    spread = jnp.einsum(
-        "iksr,arjc->ijksac", coeffs, up_factor_split, preferred_element_type=jnp.float32
-    )
-    delta = jnp.einsum("ijksac,ika->ijksc", spread, select).astype(jnp.bfloat16)
-    delta = delta.reshape(owners, count, steps, slice_part)
-    back = lax.all_to_all(delta, ("dp", "tensor"), split_axis=0, concat_axis=0, tiled=True)
-    flat_rows = inner_y.reshape(streams * steps, channel_count)
-    partial_value = jnp.dot(flat_rows, output_projection, preferred_element_type=jnp.float32)
-    total = lax.psum_scatter(
-        partial_value.reshape(streams, steps, width), "tensor", scatter_dimension=2, tiled=True
-    )
-    carried = jnp.dot(
-        dispatch.T,
-        back.reshape(owners * capacity, steps * slice_part),
-        preferred_element_type=jnp.float32,
-    )
-    layer_out = (total + carried.reshape(streams, steps, slice_part)).astype(jnp.bfloat16)
+    if small:
+        spread = jnp.einsum(
+            "iksr,arc->iksac", coeffs, adapter_up_factor, preferred_element_type=jnp.float32
+        )
+        delta = jnp.einsum("iksac,ika->iksc", spread, select).astype(jnp.bfloat16)
+        back = lax.all_to_all(delta, "dp", split_axis=0, concat_axis=0, tiled=True)
+        mine = lax.axis_index("tensor")
+        near = lax.dynamic_index_in_dim(
+            dispatch.reshape(n_dp, tensor_parts, capacity, streams), mine, 1, keepdims=False
+        )
+        carried = jnp.dot(
+            near.reshape(n_dp * capacity, streams).T,
+            back.reshape(n_dp * capacity, steps * width),
+            preferred_element_type=jnp.float32,
+        )
+        flat_rows = inner_y.reshape(streams * steps, channel_count)
+        partial_value = jnp.dot(flat_rows, output_projection, preferred_element_type=jnp.float32)
+        partial_value = partial_value + carried.reshape(streams * steps, width)
+        total = scattered(partial_value.astype(jnp.bfloat16), tensor_parts)
+        layer_out = total.reshape(streams, steps, slice_part)
+    else:
+        up_factor_split = adapter_up_factor.reshape(owner_share, rank_width, tensor_parts, slice_part)
+        spread = jnp.einsum(
+            "iksr,arjc->ijksac", coeffs, up_factor_split, preferred_element_type=jnp.float32
+        )
+        delta = jnp.einsum("ijksac,ika->ijksc", spread, select).astype(jnp.bfloat16)
+        delta = delta.reshape(owners, count, steps, slice_part)
+        back = lax.all_to_all(delta, ("dp", "tensor"), split_axis=0, concat_axis=0, tiled=True)
+        flat_rows = inner_y.reshape(streams * steps, channel_count)
+        partial_value = jnp.dot(flat_rows, output_projection, preferred_element_type=jnp.float32)
+        total = lax.psum_scatter(
+            partial_value.reshape(streams, steps, width), "tensor", scatter_dimension=2, tiled=True
+        )
+        carried = jnp.dot(
+            dispatch.T,
+            back.reshape(owners * capacity, steps * slice_part),
+            preferred_element_type=jnp.float32,
+        )
+        layer_out = (total + carried.reshape(streams, steps, slice_part)).astype(jnp.bfloat16)
     return (layer_out, state)
 
 

time: 301 us -> 195 us (0.65)
  waiting for transfers between devices: 165 us -> 28.1 us
  Pallas kernels: 0 us -> 67.5 us
  blocking collectives: 23.6 us -> 4.96 us
  between operations: 14.4 us -> 0.95 us
  matrix products: 42 us -> 36.7 us
    psum x1 -> x0, waiting for transfers between devices: 71.7 us -> none  [body(): projected = lax.psum(partial_proj, 'tensor')]
    pallas_call x0 -> x2, Pallas kernels: none -> 67.5 us  [the longest x1 45.3 us: scattered(): pl.pallas_call(scatter_kernel, out_shape=jax.ShapeDtypeStruct((rows, own)...]
    all_to_all x1, waiting for transfers between devices: 63.7 us -> 28.1 us  [body(): lax.all_to_all(outgoing, ('dp', 'tensor'), split_axis=0, concat_axis=0, t...]
    reduce_scatter x1 -> x0, waiting for transfers between devices: 27.1 us -> none  [body(): lax.psum_scatter(partial_value.reshape(streams, steps, width), 'tensor',...]
    all_to_all x1, blocking collectives: 23.6 us -> 4.96 us  [body(): back = lax.all_to_all(delta, 'dp', split_axis=0, concat_axis=0, tiled=True)]
    reshape x1 -> x3, local copies, waits for them, and re-layouts: 1.49 us -> 7.28 us  [the longest x1 6.35 us: body(): partial_value = partial_value + carried.reshape(streams * steps, width)]
    dot_general x3 -> x1, matrix products: 4.46 us -> 1.03 us  [body(): jnp.dot(conv_low, input_coefficient_projection, preferred_element_type=jn...]
    unnamed x57 -> x29, local copies, waits for them, and re-layouts: 12.6 us -> 11.5 us
  transfers between devices with their start and end apart: 4 -> 2, of which waited for: 4 -> 1; matrix products, arithmetic and copies ran while one was open for 10% -> 17% of each run, Pallas kernels for 0% -> 11%
where the time goes in v1:
time: 195 us; the launch traced here: 194 us
  Pallas kernels  67.5 us (35%)
  matrix products  36.7 us (19%)
  waiting for transfers between devices  28.1 us (14%)
  local copies, waits for them, and re-layouts  22.3 us (11%)
  other arithmetic  18 us (9%)
  starting transfers between devices  15.4 us (8%)
  blocking collectives  4.96 us (3%)
    pallas_call x1, Pallas kernels, scattered(): pl.pallas_call(scatter_kernel, out_shape=jax.ShapeDtypeStruct((rows, own)...  45.3 us
    all_to_all x1, waiting for transfers between devices, body(): lax.all_to_all(outgoing, ('dp', 'tensor'), split_axis=0, concat_axis=0, t...  28.1 us
    pallas_call x1, Pallas kernels, summed_and_normed(): pl.pallas_call(functools.partial(norm_kernel, parts, dt_rank), out_shape=...  22.2 us
    dot_general x1, matrix products, body(): jnp.dot(flat_rows, output_projection, preferred_element_type=jnp.float32)  17.6 us
    reduce_sum x1, other arithmetic, body(): jnp.sum(state * out_coef[:, :, None], axis=1) + channel_skip_gain * conv_out  14 us
    unnamed x29, local copies, waits for them, and re-layouts  11.5 us
    all_to_all x1, starting transfers between devices, body(): lax.all_to_all(outgoing, ('dp', 'tensor'), split_axis=0, concat_axis=0, t...  8.81 us
    dot_general x1, matrix products, body(): jnp.einsum('itksc,atcr->iksar', rows, down_factor, preferred_element_type...  7.35 us
  transfers between devices with their start and end apart: 2, of which 1 were waited for; matrix products, arithmetic and copies ran while one was open for 17% of the time, Pallas kernels for 11%

profile of v1, /device:TPU:9, one launch (start us, length us, event | category | flops | bytes accessed | tf_op | source)
XLA Modules:
  0.0 194.0 jit_solution(6135636632678492448)
XLA Ops:
  0.7 0.8 and_select_fusion
  1.8 0.7 all_to_all.13
  2.5 6.6 %all-to-all-start.1 = ((s32[16,1,8]{2,1,0:T(1,128)}), s32[16,1,8]{2,1,0:T(1,128)S(1)}, u32[]{:S(2)}, u32[]{:S(2)}) async-start(s32[16,1,8]{2,1,0:T(1,128)} %bitcast.17), calls=%async_computation.1 | async-start | bytes 16384 | tf_op jit(solution)/shard_map/all_to_all | solution.py:285
  9.1 1.2 constant_dynamic-update-slice_fusion.1
  10.3 1.2 constant_dynamic-update-slice_fusion
  11.5 1.5 multiply_reduce_fusion.5
  13.0 0.5 fusion.53
  13.5 1.0 fusion.13
  14.5 22.2 %shard_map.167 = (bf16[8,32,512]{2,1,0:T(8,128)(2,1)S(1)}, f32[8,24,32]{2,1,0:T(8,128)S(1)}) custom-call(f32[8,24,544]{2,1,0:T(8,128)S(1)} %bitcast.95, f32[1,512]{1,0:T(1,128)S(1)} %bitcast.97), custom_call_target="tpu_custom_call" | custom-call | tf_op jit(solution)/shard_map/pallas_call | solution.py:71
  36.8 0.7 fusion.59
  37.5 0.7 fusion.58
  38.2 0.7 fusion.57
  39.1 14.0 %multiply_reduce_fusion.2 = (f32[64,2048]{1,0:T(8,128)S(1)}, f32[64,2048]{1,0:T(8,128)S(1)}, f32[64,2048]{1,0:T(8,128)S(1)}, f32[64,16,2048]{2,1,0:T(8,128)}) fusion(f32[64,16,2048]{2,1,0:T(8,128)S(1)} %bitcast.99, f32[64,16]{1,0:T(8,128)S(1)} %get-tuple-element.40, f32[64,2048]{1,0:T(8,128)S(1)} %get-tuple-element.24, f32[64,16]{1,0:T(8,128)S(1)} %get-tuple-element.41, ...), kind=kLoop, calls=%fused_computation.6 | loop fusion | flops 43646976 | bytes 23224320 | tf_op jit(solution)/shard_map/reduce_sum | solution.py:264
  53.1 0.8 fusion.33
  54.1 1.9 convolution_convert_fusion
  56.0 8.8 %all-to-all-start = ((bf16[16,8,3,2048]{3,1,2,0:T(8,128)(2,1)}), bf16[16,8,3,2048]{3,1,2,0:T(8,128)(2,1)}, u32[]{:S(2)}, u32[]{:S(2)}) async-start(bf16[16,8,3,2048]{3,1,2,0:T(8,128)(2,1)} %bitcast.11), calls=%async_computation | async-start | bytes 3145728 | tf_op jit(solution)/shard_map/all_to_all | solution.py:284
  64.8 7.3 %copy.67 = bf16[16,8,8,2048]{3,2,1,0:T(8,128)(2,1)} copy(bf16[16,8,8,2048]{3,1,2,0:T(8,128)(2,1)} %bitcast.100) | data formatting | bytes 8388608
  72.1 0.7 copy.41
  72.8 0.7 reshape.326
  73.6 28.1 %all-to-all-done = bf16[16,8,3,2048]{3,1,2,0:T(8,128)(2,1)} async-done(((bf16[16,8,3,2048]{3,1,2,0:T(8,128)(2,1)}), bf16[16,8,3,2048]{3,1,2,0:T(8,128)(2,1)}, u32[]{:S(2)}, u32[]{:S(2)}) %all-to-all-start) | async-done | bytes 1572896 | tf_op jit(solution)/shard_map/all_to_all | solution.py:284
  101.7 7.4 %fusion.8 = bf16[2,8,3,2,64]{4,1,3,2,0:T(8,128)(2,1)S(1)} fusion(bf16[2,8,2048,64,1,1]{2,1,3,0,5,4:T(8,128)(2,1)} %bitcast.101, bf16[2,8,8,3,2048,1]{4,2,3,1,0,5:T(8,128)(2,1)} %bitcast.13), kind=kOutput, calls=%fused_computation.26 | convolution fusion | flops 201326592 | bytes 5779456 | tf_op jit(solution)/shard_map/itksc,atcr->iksar/dot_general | solution.py:290
  109.3 0.6 fusion.5
  109.8 2.3 %fusion.3 = bf16[2,8,1,3,8192]{4,2,3,1,0:T(2,128)(2,1)S(1)} fusion(bf16[2,8,3,2,8192]{4,1,3,2,0:T(8,128)(2,1)S(1)} %fusion.5, pred[2,8,2,1,1]{2,1,0,3,4:T(8,128)(4,1)S(1)} %fusion.45), kind=kOutput, calls=%fused_computation.11 | convolution fusion | flops 1572864 | bytes 2359328 | tf_op jit(solution)/shard_map/iksac,ika->iksc/dot_general | solution.py:296
  112.2 0.9 copy.89
  113.0 5.0 %all_to_all.19 = bf16[2,8,3,8192]{3,1,2,0:T(8,128)(2,1)S(1)} all-to-all(bf16[2,8,3,8192]{3,1,2,0:T(8,128)(2,1)S(1)} %bitcast.103), channel_id=1, replica_groups=mesh['groups'=2,'dp'=2,'tensor'=8] {'dp'}, dimensions={0} | all-to-all | bytes 1572864 | tf_op jit(solution)/shard_map/all_to_all | solution.py:297
  118.0 3.7 %fusion.46 = f32[64,24576]{1,0:T(8,128)} fusion(bf16[16,24576]{1,0:T(8,128)(2,1)S(1)} %bitcast.104, s32[64]{0:T(128)S(1)} %multiply_add_fusion.4, s32[2,1,8]{2,1,0:T(1,128)S(1)} %constant_dynamic-slice_fusion), kind=kOutput, calls=%fused_computation.82 | convolution fusion | flops 50332672 | bytes 7078208 | tf_op jit(solution)/shard_map/dot_general | solution.py:302
  121.7 6.3 %reshape.334 = f32[192,8192]{1,0:T(8,128)} reshape(f32[64,24576]{1,0:T(8,128)} %fusion.46) | data formatting | bytes 12582912 | tf_op jit(solution)/shard_map/reshape | solution.py:309
  128.1 17.6 %fusion.x_ref = bf16[192,8192]{1,0:T(8,128)(2,1)} fusion(f32[192,8192]{1,0:T(8,128)} %reshape.334, bf16[192,2048]{1,0:T(8,128)(2,1)S(1)} %reshape.326, bf16[2048,8192]{1,0:T(8,128)(2,1)} %param.29), kind=kOutput, calls=%fused_computation.1 | convolution fusion | flops 6445596672 | bytes 43778048 | tf_op jit(solution)/shard_map/dot_general | solution.py:308
  145.7 1.9 copy-done.2
  147.6 45.3 %shard_map.168 = bf16[192,1024]{1,0:T(8,128)(2,1)S(1)} custom-call(bf16[192,8192]{1,0:T(8,128)(2,1)S(1)} %copy-done.2), custom_call_target="tpu_custom_call" | custom-call | tf_op jit(solution)/shard_map/pallas_call | solution.py:179
  192.9 0.2 reshape.335
  193.1 0.9 copy.48
  (39 shorter events, 1.0 us)
Async XLA Ops:
  0.6 12.8 %copy-start = (bf16[2048,544]{0,1:T(8,128)(2,1)S(1)}, bf16[2048,544]{0,1:T(8,128)(2,1)}, u32[]{:S(2)}) copy-start(bf16[2048,544]{0,1:T(8,128)(2,1)} %param.23) | copy-start | bytes 6684676
  0.6 12.3 %copy-start.8 = (f32[2048]{0:T(1024)S(1)}, f32[2048]{0:T(1024)}, u32[]{:S(2)}) copy-start(f32[2048]{0:T(1024)} %param.22) | copy-start | bytes 24580
  2.5 53.5 %all-to-all-start.1 = ((s32[16,1,8]{2,1,0:T(1,128)}), s32[16,1,8]{2,1,0:T(1,128)S(1)}, u32[]{:S(2)}, u32[]{:S(2)}) async-start(s32[16,1,8]{2,1,0:T(1,128)} %bitcast.17), calls=%async_computation.1 | async-start | bytes 16384 | tf_op jit(solution)/shard_map/all_to_all | solution.py:285
  12.9 1.6 copy-start.3
  12.9 23.8 %copy-start.4 = (bf16[512,2048]{1,0:T(8,128)(2,1)S(1)}, bf16[512,2048]{1,0:T(8,128)(2,1)}, u32[]{:S(2)}) copy-start(bf16[512,2048]{1,0:T(8,128)(2,1)} %param.25) | copy-start | bytes 6291460
  13.0 23.8 %copy-start.7 = (f32[2048]{0:T(1024)S(1)}, f32[2048]{0:T(1024)}, u32[]{:S(2)}) copy-start(f32[2048]{0:T(1024)} %param.26) | copy-start | bytes 24580
  13.4 25.5 %slice-start = ((s8[8388608]{0:T(1024)(128)(4,1)}), s8[4194304]{0:T(1024)(128)(4,1)S(1)}, s32[]{:S(2)}) async-start(s8[8388608]{0:T(1024)(128)(4,1)} %bitcast.98), calls=%async_computation.3 | async-start | bytes 8388608
  36.8 2.2 %slice-start.1 = ((s8[8388608]{0:T(1024)(128)(4,1)}), s8[4194304]{0:T(1024)(128)(4,1)S(1)}, s32[]{:S(2)}) async-start(s8[8388608]{0:T(1024)(128)(4,1)} %bitcast.98), calls=%async_computation.4 | async-start | bytes 8388608
  37.5 1.6 copy-start.6
  39.1 14.0 %copy-start.5 = (bf16[64,3,2048]{2,0,1:T(8,128)(2,1)S(1)}, bf16[64,3,2048]{2,0,1:T(8,128)(2,1)}, u32[]{:S(2)}) copy-start(bf16[64,3,2048]{2,0,1:T(8,128)(2,1)} %param.17) | copy-start | bytes 2359300
  39.1 14.0 %copy-start.9 = (f32[2048]{0:T(1024)S(1)}, f32[2048]{0:T(1024)}, u32[]{:S(2)}) copy-start(f32[2048]{0:T(1024)} %param.28) | copy-start | bytes 24580
  56.0 45.7 %all-to-all-start = ((bf16[16,8,3,2048]{3,1,2,0:T(8,128)(2,1)}), bf16[16,8,3,2048]{3,1,2,0:T(8,128)(2,1)}, u32[]{:S(2)}, u32[]{:S(2)}) async-start(bf16[16,8,3,2048]{3,1,2,0:T(8,128)(2,1)} %bitcast.11), calls=%async_computation | async-start | bytes 3145728 | tf_op jit(solution)/shard_map/all_to_all | solution.py:284
  101.7 7.5 %copy-start.10 = (bf16[2,64,8192]{2,1,0:T(8,128)(2,1)S(1)}, bf16[2,64,8192]{2,1,0:T(8,128)(2,1)}, u32[]{:S(2)}) copy-start(bf16[2,64,8192]{2,1,0:T(8,128)(2,1)} %param.31) | copy-start | bytes 6291460
  128.1 66.0 %copy-start.1 = (bf16[2048,544]{0,1:T(8,128)(2,1)S(1)}, bf16[2048,544]{0,1:T(8,128)(2,1)}, u32[]{:S(2)}) copy-start(bf16[2048,544]{0,1:T(8,128)(2,1)} %param.23) | copy-start | bytes 6684676
  145.7 1.9 copy-start.2

commit v2 on v1

--- a/solution.py
+++ b/solution.py
@@ -87,7 +87,7 @@
     return dt[:, :share].reshape(rows, dt_rank), coef.reshape(rows, columns - dt_rank)
 
 
-def scatter_kernel(x_ref, out_ref, r0, r1, r2, a1, a2, send_sem, recv_sem):
+def scatter_kernel(base_ref, spot_ref, back_ref, out_ref, x_ref, r0, r1, r2, a1, a2, send_sem, recv_sem):
     me = lax.axis_index("tensor")
     y, z = lax.rem(me, 2), me // 2
     h = z // 2
@@ -124,6 +124,11 @@
     def columns(flow, sel):
         return pl.ds(pl.multiple_of(place(sel) * width + flow * half, 128), half)
 
+    def block(flow, sel):
+        where = columns(flow, sel)
+        extra = jnp.dot(spot_ref[...], back_ref[:, where], preferred_element_type=jnp.float32)
+        return base_ref[:, where] + extra
+
     def chosen(order, values):
         sel = [None] * 3
         for d, v in zip(order, values):
@@ -137,13 +142,15 @@
                 o = orders[flow]
                 b1 = 1 - bits[o[1]] if p == 0 else bits[o[1]]
                 sel = chosen(o, (1 - bits[o[0]], b1, q))
-                first[flow].append(send(flow, p * 2 + q, x_ref.at[:, columns(flow, sel)], r0.at[flow, p * 2 + q], o[0]))
+                n = p * 2 + q
+                x_ref[flow, n] = block(flow, sel).astype(jnp.bfloat16)
+                first[flow].append(send(flow, n, x_ref.at[flow, n], r0.at[flow, n], o[0]))
     for q in range(2):
         for flow in range(2):
             o = orders[flow]
             first[flow][q].wait_recv()
             sel = chosen(o, (bits[o[0]], 1 - bits[o[1]], q))
-            own = x_ref[:, columns(flow, sel)].astype(jnp.float32)
+            own = block(flow, sel)
             a1[flow, q] = (own + r0[flow, q].astype(jnp.float32)).astype(jnp.bfloat16)
             second[flow].append(send(flow, 4 + q, a1.at[flow, q], r1.at[flow, q], o[1]))
     for q in range(2):
@@ -151,7 +158,7 @@
             o = orders[flow]
             first[flow][2 + q].wait_recv()
             sel = chosen(o, (bits[o[0]], bits[o[1]], q))
-            own = x_ref[:, columns(flow, sel)].astype(jnp.float32)
+            own = block(flow, sel)
             a2[flow, q] = own + r0[flow, 2 + q].astype(jnp.float32)
     for flow in range(2):
         o = orders[flow]
@@ -172,16 +179,17 @@
             copy.wait_send()
 
 
-def scattered(partial, parts):
-    rows, width = partial.shape
+def scattered(base, spot, back, parts):
+    rows, width = base.shape
     own = width // parts
     half = own // 2
     return pl.pallas_call(
         scatter_kernel,
         out_shape=jax.ShapeDtypeStruct((rows, own), jnp.bfloat16),
-        in_specs=[pl.BlockSpec(memory_space=pltpu.VMEM)],
+        in_specs=[pl.BlockSpec(memory_space=pltpu.VMEM)] * 3,
         out_specs=pl.BlockSpec(memory_space=pltpu.VMEM),
         scratch_shapes=[
+            pltpu.VMEM((2, 4, rows, half), jnp.bfloat16),
             pltpu.VMEM((2, 4, rows, half), jnp.bfloat16),
             pltpu.VMEM((2, 2, rows, half), jnp.bfloat16),
             pltpu.VMEM((2, rows, half), jnp.bfloat16),
@@ -193,7 +201,149 @@
         compiler_params=pltpu.CompilerParams(
             collective_id=1, has_side_effects=True, vmem_limit_bytes=32 << 20
         ),
-    )(partial)
+    )(base, spot, back)
+
+
+def dispatch_kernel(n_dp, parts, x_ref, outgoing_ref, down_ref, w_ref, base_ref, coef_ref, held, total, send_sem, recv_sem):
+    owners = n_dp * parts
+    me = lax.axis_index("dp") * parts + lax.axis_index("tensor")
+
+    def device(peer):
+        return {"dp": peer // parts, "tensor": lax.rem(peer, parts)}
+
+    barrier = pltpu.get_barrier_semaphore()
+    for k in range(1, owners):
+        peer = lax.rem(me + k, owners)
+        pl.semaphore_signal(barrier, inc=1, device_id=device(peer), device_id_type=MESH)
+    pl.semaphore_wait(barrier, owners - 1)
+    copies = []
+    for k in range(1, owners):
+        peer = lax.rem(me + k, owners)
+        copy = pltpu.make_async_remote_copy(
+            src_ref=outgoing_ref.at[peer],
+            dst_ref=held.at[k - 1],
+            send_sem=send_sem.at[k - 1],
+            recv_sem=recv_sem.at[k - 1],
+            device_id=device(peer),
+            device_id_type=MESH,
+        )
+        copy.start()
+        copies.append(copy)
+    rows, depth = x_ref.shape
+    tile = 512
+
+    def multiply(w_tile, base_tile):
+        base_tile[...] = jnp.dot(x_ref[...], w_tile[...], preferred_element_type=jnp.float32)
+
+    pltpu.emit_pipeline(
+        multiply,
+        grid=(w_ref.shape[1] // tile,),
+        in_specs=[pl.BlockSpec((depth, tile), lambda j: (0, j))],
+        out_specs=[pl.BlockSpec((rows, tile), lambda j: (0, j))],
+    )(w_ref, base_ref)
+    half = depth // 2
+    lines = held.shape[1] // 2
+    total[...] = jnp.zeros_like(total)
+    for k in range(owners):
+        source = lax.rem(me - k + owners, owners)
+        part = lax.rem(source, parts)
+        if k:
+            copies[k - 1].wait_recv()
+            rows_in = held[k - 1]
+        else:
+            rows_in = outgoing_ref[me]
+        found = []
+        for side in range(2):
+            where = pl.ds(pl.multiple_of(part * depth + side * half, 128), half)
+            found.append(
+                lax.dot_general(
+                    rows_in, down_ref[:, where], (((1,), (1,)), ((), ())), preferred_element_type=jnp.float32
+                )
+            )
+        total[source // parts] += found[0][:lines] + found[1][lines:]
+    coef_ref[...] = total[...]
+    for copy in copies:
+        copy.wait_send()
+
+
+def dispatched(x, outgoing, down, w, n_dp, parts):
+    owners, lines, half = outgoing.shape
+    dma = pltpu.SemaphoreType.DMA((owners - 1,))
+    return pl.pallas_call(
+        functools.partial(dispatch_kernel, n_dp, parts),
+        out_shape=(
+            jax.ShapeDtypeStruct((x.shape[0], w.shape[1]), jnp.float32),
+            jax.ShapeDtypeStruct((n_dp, lines // 2, down.shape[0]), jnp.float32),
+        ),
+        in_specs=[pl.BlockSpec(memory_space=pltpu.VMEM)] * 3 + [pl.BlockSpec(memory_space=pl.ANY)],
+        out_specs=(pl.BlockSpec(memory_space=pl.ANY), pl.BlockSpec(memory_space=pltpu.VMEM)),
+        scratch_shapes=[
+            pltpu.VMEM((owners - 1, lines, half), jnp.bfloat16),
+            pltpu.VMEM((n_dp, lines // 2, down.shape[0]), jnp.float32),
+            dma,
+            dma,
+        ],
+        compiler_params=pltpu.CompilerParams(
+            collective_id=2, has_side_effects=True, vmem_limit_bytes=40 << 20
+        ),
+    )(x, outgoing, down, w)
+
+
+def slots_of(index, owner_share, owners, capacity):
+    streams = index.shape[0]
+    owner = index // owner_share
+    position = jnp.arange(streams, dtype=jnp.int32)
+    before = (owner[:, None] == owner[None, :]) & (position[None, :] < position[:, None])
+    slot = owner * capacity + jnp.sum(before.astype(jnp.int32), axis=1)
+    return jnp.arange(owners * capacity, dtype=jnp.int32)[:, None] == slot[None, :]
+
+
+def adapted(x, index, sibling_index, down_factor, up_factor, w, capacity, steps):
+    n_dp = lax.axis_size("dp")
+    parts = lax.axis_size("tensor")
+    owners = n_dp * parts
+    streams = index.shape[0]
+    owner_share, channels, rank = down_factor.shape
+    width = w.shape[1]
+    group, mine = lax.axis_index("dp"), lax.axis_index("tensor")
+    match = slots_of(index, owner_share, owners, capacity)
+    same = jnp.eye(steps, dtype=jnp.bool_)
+    spread_out = (
+        match.reshape(owners, 1, capacity, 1, streams) & same[None, :, None, :, None]
+    ).astype(jnp.bfloat16).reshape(owners, steps * capacity, steps * streams)
+    flat = spread_out.reshape(owners * steps * capacity, steps * streams)
+    half = x.shape[1] // 2
+    sides = [
+        jnp.dot(flat, x[:, side * half : (side + 1) * half], preferred_element_type=jnp.float32)
+        .astype(jnp.bfloat16)
+        .reshape(owners, steps * capacity, half)
+        for side in range(2)
+    ]
+    outgoing = jnp.concatenate(sides, axis=1)
+    down = jnp.transpose(down_factor, (0, 2, 1)).reshape(owner_share * rank, channels)
+    base, coef = dispatched(x, outgoing, down, w, n_dp, parts)
+    me = group * parts + mine
+    keeps = []
+    for source in range(n_dp):
+        held = jnp.where(group == source, index, sibling_index)
+        match_in = slots_of(held, owner_share, owners, capacity).reshape(owners, capacity, streams)
+        match_in = lax.dynamic_index_in_dim(match_in, me, 0, keepdims=False)
+        local = jnp.sum(jnp.where(match_in, (held % owner_share)[None, :], 0), axis=1)
+        keep = local[:, None] == jnp.arange(owner_share, dtype=jnp.int32)[None, :]
+        keeps.append(jnp.tile(jnp.repeat(keep, rank, axis=1), (steps, 1)))
+    coeffs = jnp.where(jnp.stack(keeps), coef, 0.0).astype(jnp.bfloat16)
+    delta = jnp.dot(
+        coeffs.reshape(n_dp * steps * capacity, owner_share * rank),
+        up_factor.reshape(owner_share * rank, width),
+        preferred_element_type=jnp.float32,
+    ).astype(jnp.bfloat16)
+    delta = delta.reshape(n_dp, steps * capacity, width)
+    back = lax.all_to_all(delta, "dp", split_axis=0, concat_axis=0, tiled=True)
+    spot = lax.dynamic_index_in_dim(
+        spread_out.reshape(n_dp, parts, steps * capacity, steps * streams), mine, 1, keepdims=False
+    ).reshape(n_dp * steps * capacity, steps * streams).T
+    total = scattered(base, spot, back.reshape(n_dp * steps * capacity, width), parts)
+    return jnp.transpose(total.reshape(steps, streams, width // parts), (1, 0, 2))
 
 
 def body(
@@ -264,6 +414,19 @@
         read = jnp.sum(state * out_coef[:, :, None], axis=1) + channel_skip_gain * conv_out
         gated = read * jax.nn.silu(gate_branch_input[:, step].astype(jnp.float32))
         gathered.append(gated.astype(jnp.bfloat16))
+    if small:
+        sibling_index = lax.ppermute(stream_adapter_index, "dp", ((0, 1), (1, 0)))
+        layer_out = adapted(
+            jnp.concatenate(gathered, axis=0),
+            stream_adapter_index,
+            sibling_index,
+            adapter_down_factor,
+            adapter_up_factor,
+            output_projection,
+            capacity,
+            steps,
+        )
+        return (layer_out, state)
     inner_y = jnp.stack(gathered, axis=1)
     owner = stream_adapter_index // owner_share
     local = stream_adapter_index % owner_share
@@ -289,45 +452,24 @@
     select = (which[..., None] == jnp.arange(owner_share, dtype=jnp.int32)).astype(jnp.float32)
     every = jnp.einsum("itksc,atcr->iksar", rows, down_factor, preferred_element_type=jnp.float32)
     coeffs = jnp.einsum("iksar,ika->iksr", every, select).astype(jnp.bfloat16)
-    if small:
-        spread = jnp.einsum(
-            "iksr,arc->iksac", coeffs, adapter_up_factor, preferred_element_type=jnp.float32
-        )
-        delta = jnp.einsum("iksac,ika->iksc", spread, select).astype(jnp.bfloat16)
-        back = lax.all_to_all(delta, "dp", split_axis=0, concat_axis=0, tiled=True)
-        mine = lax.axis_index("tensor")
-        near = lax.dynamic_index_in_dim(
-            dispatch.reshape(n_dp, tensor_parts, capacity, streams), mine, 1, keepdims=False
-        )
-        carried = jnp.dot(
-            near.reshape(n_dp * capacity, streams).T,
-            back.reshape(n_dp * capacity, steps * width),
-            preferred_element_type=jnp.float32,
-        )
-        flat_rows = inner_y.reshape(streams * steps, channel_count)
-        partial_value = jnp.dot(flat_rows, output_projection, preferred_element_type=jnp.float32)
-        partial_value = partial_value + carried.reshape(streams * steps, width)
-        total = scattered(partial_value.astype(jnp.bfloat16), tensor_parts)
-        layer_out = total.reshape(streams, steps, slice_part)
-    else:
-        up_factor_split = adapter_up_factor.reshape(owner_share, rank_width, tensor_parts, slice_part)
-        spread = jnp.einsum(
-            "iksr,arjc->ijksac", coeffs, up_factor_split, preferred_element_type=jnp.float32
-        )
-        delta = jnp.einsum("ijksac,ika->ijksc", spread, select).astype(jnp.bfloat16)
-        delta = delta.reshape(owners, count, steps, slice_part)
-        back = lax.all_to_all(delta, ("dp", "tensor"), split_axis=0, concat_axis=0, tiled=True)
-        flat_rows = inner_y.reshape(streams * steps, channel_count)
-        partial_value = jnp.dot(flat_rows, output_projection, preferred_element_type=jnp.float32)
-        total = lax.psum_scatter(
-            partial_value.reshape(streams, steps, width), "tensor", scatter_dimension=2, tiled=True
-        )
-        carried = jnp.dot(
-            dispatch.T,
-            back.reshape(owners * capacity, steps * slice_part),
-            preferred_element_type=jnp.float32,
-        )
-        layer_out = (total + carried.reshape(streams, steps, slice_part)).astype(jnp.bfloat16)
+    up_factor_split = adapter_up_factor.reshape(owner_share, rank_width, tensor_parts, slice_part)
+    spread = jnp.einsum(
+        "iksr,arjc->ijksac", coeffs, up_factor_split, preferred_element_type=jnp.float32
+    )
+    delta = jnp.einsum("ijksac,ika->ijksc", spread, select).astype(jnp.bfloat16)
+    delta = delta.reshape(owners, count, steps, slice_part)
+    back = lax.all_to_all(delta, ("dp", "tensor"), split_axis=0, concat_axis=0, tiled=True)
+    flat_rows = inner_y.reshape(streams * steps, channel_count)
+    partial_value = jnp.dot(flat_rows, output_projection, preferred_element_type=jnp.float32)
+    total = lax.psum_scatter(
+        partial_value.reshape(streams, steps, width), "tensor", scatter_dimension=2, tiled=True
+    )
+    carried = jnp.dot(
+        dispatch.T,
+        back.reshape(owners * capacity, steps * slice_part),
+        preferred_element_type=jnp.float32,
+    )
+    layer_out = (total + carried.reshape(streams, steps, slice_part)).astype(jnp.bfloat16)
     return (layer_out, state)
 
 

time: 195 us -> 157 us (0.81)
  Pallas kernels: 67.5 us -> 111 us
  matrix products: 36.7 us -> 6.87 us
  waiting for transfers between devices: 28.1 us -> 1.03 us
  starting transfers between devices: 15.4 us -> 4.92 us
  local copies, waits for them, and re-layouts: 22.3 us -> 12.9 us
  blocking collectives: 4.96 us -> 0 us
    pallas_call x0 -> x1, Pallas kernels: none -> 40.4 us  [dispatched(): pl.pallas_call(functools.partial(dispatch_kernel, n_dp, parts), out_shape...]
    dot_general x7 -> x3, matrix products: 33.6 us -> 2.03 us  [the longest x1 1.31 us: adapted(): jnp.dot(coeffs.reshape(n_dp * steps * capacity, owner_share * rank), up_f...]
    all_to_all x2 -> x1, waiting for transfers between devices: 28.1 us -> 1.03 us  [adapted(): back = lax.all_to_all(delta, 'dp', split_axis=0, concat_axis=0, tiled=True)]
    all_to_all x2 -> x1, starting transfers between devices: 15.4 us -> 4.18 us  [adapted(): back = lax.all_to_all(delta, 'dp', split_axis=0, concat_axis=0, tiled=True)]
    reshape x4 -> x1, local copies, waits for them, and re-layouts: 7.33 us -> 0.11 us  [adapted(): spot = lax.dynamic_index_in_dim(spread_out.reshape(n_dp, parts, steps * c...]
    all_to_all x1 -> x0, blocking collectives: 4.96 us -> none  [body(): back = lax.all_to_all(delta, 'dp', split_axis=0, concat_axis=0, tiled=True)]
    pallas_call x1, Pallas kernels: 45.3 us -> 48.2 us  [scattered(): pl.pallas_call(scatter_kernel, out_shape=jax.ShapeDtypeStruct((rows, own)...]
    unnamed x29 -> x34, local copies, waits for them, and re-layouts: 11.5 us -> 9.75 us
  transfers between devices with their start and end apart: 2 -> 2, of which waited for: 1 -> 1; matrix products, arithmetic and copies ran while one was open for 17% -> 17% of each run, Pallas kernels for 11% -> 14%
where the time goes in v2:
time: 157 us
  Pallas kernels  111 us (71%)
  other arithmetic  18.8 us (12%)
  local copies, waits for them, and re-layouts  12.9 us (8%)
  matrix products  6.87 us (4%)
  starting transfers between devices  4.92 us (3%)
    pallas_call x1, Pallas kernels, scattered(): pl.pallas_call(scatter_kernel, out_shape=jax.ShapeDtypeStruct((rows, own)...  48.2 us
    pallas_call x1, Pallas kernels, dispatched(): pl.pallas_call(functools.partial(dispatch_kernel, n_dp, parts), out_shape...  40.4 us
    pallas_call x1, Pallas kernels, summed_and_normed(): pl.pallas_call(functools.partial(norm_kernel, parts, dt_rank), out_shape=...  22.5 us
    reduce_sum x1, other arithmetic, body(): jnp.sum(state * out_coef[:, :, None], axis=1) + channel_skip_gain * conv_out  15.2 us
    unnamed x34, local copies, waits for them, and re-layouts  9.75 us
    all_to_all x1, starting transfers between devices, adapted(): back = lax.all_to_all(delta, 'dp', split_axis=0, concat_axis=0, tiled=True)  4.18 us
    dot_general x3, matrix products, body(): jnp.dot(dt_low, step_size_projection, preferred_element_type=jnp.float32)  3.81 us
  transfers between devices with their start and end apart: 2, of which 1 were waited for; matrix products, arithmetic and copies ran while one was open for 17% of the time, Pallas kernels for 14%

profile of v2, /device:TPU:9, one launch (start us, length us, event | category | flops | bytes accessed | tf_op | source)
XLA Modules:
  0.0 156.6 jit_solution(9554925352869119989)
XLA Ops:
  0.7 0.7 collective-permute-start
  1.4 1.2 constant_dynamic-update-slice_fusion.1
  2.6 1.2 constant_dynamic-update-slice_fusion
  3.8 0.5 multiply_reduce_fusion.5
  4.4 0.1 copy-done.13
  4.5 1.2 fusion.31
  5.7 1.0 fusion
  6.8 22.5 %shard_map.167 = (bf16[8,32,512]{2,1,0:T(8,128)(2,1)S(1)}, f32[8,24,32]{2,1,0:T(8,128)S(1)}) custom-call(f32[8,24,544]{2,1,0:T(8,128)S(1)} %bitcast.46, f32[1,512]{1,0:T(1,128)S(1)} %bitcast.49), custom_call_target="tpu_custom_call" | custom-call | tf_op jit(solution)/shard_map/pallas_call | solution.py:71
  29.3 0.7 fusion.35
  30.0 1.5 fusion.36
  31.5 1.7 %fusion.37 = (f32[64,2048]{1,0:T(8,128)}, f32[64,2048]{1,0:T(8,128)}) fusion(f32[2048]{0:T(1024)S(1)} %copy-done.11, bf16[512,2048]{1,0:T(8,128)(2,1)S(1)} %copy-done.6, bf16[192,512]{1,0:T(8,128)(2,1)S(1)} %bitcast.55), kind=kOutput, calls=%fused_computation.104 | convolution fusion | flops 135266304 | bytes 3219456 | tf_op jit(solution)/shard_map/dot_general | solution.py:409
  33.2 0.6 fusion.34
  33.9 15.2 %multiply_reduce_fusion.2 = (f32[64,2048]{1,0:T(8,128)S(1)}, f32[64,2048]{1,0:T(8,128)S(1)}, f32[64,2048]{1,0:T(8,128)S(1)}, f32[64,16,2048]{2,1,0:T(8,128)}) fusion(f32[64,16,2048]{2,1,0:T(8,128)} %param.19, f32[64,16]{1,0:T(8,128)S(1)} %get-tuple-element.38, f32[64,2048]{1,0:T(8,128)S(1)} %get-tuple-element.24, f32[64,16]{1,0:T(8,128)} %get-tuple-element.39, ...), kind=kLoop, calls=%fused_computation.5 | loop fusion | flops 43646976 | bytes 23224320 | tf_op jit(solution)/shard_map/reduce_sum | solution.py:414
  49.1 0.5 fusion.20
  49.9 0.2 convert_reduce_fusion
  50.2 0.3 broadcast_and_fusion
  50.4 0.3 and.66
  50.7 0.4 convolution_convert_fusion.2
  51.1 0.4 convolution_convert_fusion.1
  51.5 0.2 convert_reduce_fusion.1
  51.7 0.2 select_reduce_fusion.1
  52.4 0.2 pad_maximum_fusion.outgoing_ref
  52.6 2.2 %copy-done.4 = bf16[2,16384,64]{1,2,0:T(8,128)(2,1)S(1)} copy-done((bf16[2,16384,64]{1,2,0:T(8,128)(2,1)S(1)}, bf16[2,16384,64]{1,2,0:T(8,128)(2,1)}, u32[]{:S(2)}) %copy-start.4) | copy-done | bytes 4194328
  54.8 40.4 %shard_map.168 = (f32[192,8192]{1,0:T(8,128)S(1)}, f32[2,24,128]{2,1,0:T(8,128)S(1)}) custom-call(bf16[192,2048]{1,0:T(8,128)(2,1)S(1)} %pad_maximum_fusion.1.x_ref, bf16[16,48,1024]{2,1,0:T(8,128)(2,1)S(1)} %pad_maximum_fusion.outgoing_ref, bf16[128,16384]{1,0:T(8,128)(2,1)S(1)} %bitcast.43, bf16[2048,8192]{1,0:T(8,128)(2,1)} %w_ref.1), custom_call_target="tpu_custom_call" | custom-call | tf_op jit(solution)/shard_map/pallas_call | solution.py:272
  95.1 2.6 %copy-done.2 = f32[192,8192]{1,0:T(8,128)} copy-done((f32[192,8192]{1,0:T(8,128)}, f32[192,8192]{1,0:T(8,128)S(1)}, u32[]{:S(2)}) %copy-start.2) | copy-done | bytes 6291480
  97.8 1.3 convolution_convert_fusion
  99.1 4.2 %all-to-all-start = ((bf16[2,24,8192]{2,1,0:T(8,128)(2,1)}), bf16[2,24,8192]{2,1,0:T(8,128)(2,1)S(1)}, u32[]{:S(2)}, u32[]{:S(2)}) async-start(bf16[2,24,8192]{2,1,0:T(8,128)(2,1)} %bitcast.22), calls=%async_computation | async-start | bytes 1572864 | tf_op jit(solution)/shard_map/all_to_all | solution.py:341
  103.4 0.3 and.67
  103.8 1.0 all-to-all-done
  104.9 2.8 %copy-done.3 = f32[192,8192]{1,0:T(8,128)S(1)} copy-done((f32[192,8192]{1,0:T(8,128)S(1)}, f32[192,8192]{1,0:T(8,128)}, u32[]{:S(2)}) %copy-start.3) | copy-done | bytes 6291480
  107.6 48.2 %shard_map.169 = bf16[192,1024]{1,0:T(8,128)(2,1)S(1)} custom-call(f32[192,8192]{1,0:T(8,128)S(1)} %copy-done.3, bf16[192,48]{1,0:T(8,128)(2,1)S(1)} %bitcast.48, bf16[48,8192]{1,0:T(8,128)(2,1)S(1)} %bitcast.44), custom_call_target="tpu_custom_call" | custom-call | tf_op jit(solution)/shard_map/pallas_call | solution.py:186
  155.8 0.7 copy.25
  (54 shorter events, 1.2 us)
Async XLA Ops:
  0.6 5.1 %copy-start = (bf16[2048,544]{0,1:T(8,128)(2,1)S(1)}, bf16[2048,544]{0,1:T(8,128)(2,1)}, u32[]{:S(2)}) copy-start(bf16[2048,544]{0,1:T(8,128)(2,1)} %param.23) | copy-start | bytes 6684676
  0.6 3.1 %copy-start.12 = (f32[4,2048]{1,0:T(4,128)S(1)}, f32[4,2048]{1,0:T(4,128)}, u32[]{:S(2)}) copy-start(f32[4,2048]{1,0:T(4,128)} %param.21) | copy-start | bytes 98308
  0.7 49.2 %collective-permute-start = (s32[64]{0:T(128)}, s32[64]{0:T(128)S(1)}, u32[]{:S(2)}, u32[]{:S(2)}) collective-permute-start(s32[64]{0:T(128)} %param.20), channel_id=1, source_target_pairs={{0,8},{8,0},{1,9},{9,1},{2,10},{10,2},{3,11},{11,3},{4,12},{12,4},... | collective-permute-start | bytes 776 | tf_op jit(solution)/shard_map/ppermute | solution.py:418
  3.8 0.7 copy-start.13
  5.7 1.0 copy-start.5
  5.7 23.6 %copy-start.6 = (bf16[512,2048]{1,0:T(8,128)(2,1)S(1)}, bf16[512,2048]{1,0:T(8,128)(2,1)}, u32[]{:S(2)}) copy-start(bf16[512,2048]{1,0:T(8,128)(2,1)} %param.25) | copy-start | bytes 6291460
  5.7 23.6 %copy-start.11 = (f32[2048]{0:T(1024)S(1)}, f32[2048]{0:T(1024)}, u32[]{:S(2)}) copy-start(f32[2048]{0:T(1024)} %param.26) | copy-start | bytes 24580
  31.5 2.4 %copy-start.7 = (f32[64,2048]{1,0:T(8,128)S(1)}, f32[64,2048]{1,0:T(8,128)}, u32[]{:S(2)}) copy-start(f32[64,2048]{1,0:T(8,128)} %get-tuple-element.43) | copy-start | bytes 1572868
  31.5 2.4 %copy-start.10 = (f32[16,2048]{1,0:T(8,128)S(1)}, f32[16,2048]{1,0:T(8,128)}, u32[]{:S(2)}) copy-start(f32[16,2048]{1,0:T(8,128)} %param.27) | copy-start | bytes 393220
  33.8 15.2 %copy-start.9 = (bf16[64,3,2048]{2,0,1:T(8,128)(2,1)S(1)}, bf16[64,3,2048]{2,0,1:T(8,128)(2,1)}, u32[]{:S(2)}) copy-start(bf16[64,3,2048]{2,0,1:T(8,128)(2,1)} %param.17) | copy-start | bytes 2359300
  33.8 15.2 %copy-start.14 = (f32[2048]{0:T(1024)S(1)}, f32[2048]{0:T(1024)}, u32[]{:S(2)}) copy-start(f32[2048]{0:T(1024)} %param.28) | copy-start | bytes 24580
  49.0 0.8 copy-start.15
  52.6 2.2 %copy-start.4 = (bf16[2,16384,64]{1,2,0:T(8,128)(2,1)S(1)}, bf16[2,16384,64]{1,2,0:T(8,128)(2,1)}, u32[]{:S(2)}) copy-start(bf16[2,16384,64]{1,2,0:T(8,128)(2,1)} %param.30) | copy-start | bytes 12582916
  54.8 43.1 %copy-start.8 = (bf16[2,64,8192]{2,1,0:T(8,128)(2,1)S(1)}, bf16[2,64,8192]{2,1,0:T(8,128)(2,1)}, u32[]{:S(2)}) copy-start(bf16[2,64,8192]{2,1,0:T(8,128)(2,1)} %param.31) | copy-start | bytes 6291460
  95.1 2.7 %copy-start.2 = (f32[192,8192]{1,0:T(8,128)}, f32[192,8192]{1,0:T(8,128)S(1)}, u32[]{:S(2)}) copy-start(f32[192,8192]{1,0:T(8,128)S(1)} %get-tuple-element.8.base_ref) | copy-start | bytes 18874372
  99.1 5.7 %all-to-all-start = ((bf16[2,24,8192]{2,1,0:T(8,128)(2,1)}), bf16[2,24,8192]{2,1,0:T(8,128)(2,1)S(1)}, u32[]{:S(2)}, u32[]{:S(2)}) async-start(bf16[2,24,8192]{2,1,0:T(8,128)(2,1)} %bitcast.22), calls=%async_computation | async-start | bytes 1572864 | tf_op jit(solution)/shard_map/all_to_all | solution.py:341
  104.9 2.8 %copy-start.3 = (f32[192,8192]{1,0:T(8,128)S(1)}, f32[192,8192]{1,0:T(8,128)}, u32[]{:S(2)}) copy-start(f32[192,8192]{1,0:T(8,128)} %copy-done.2) | copy-start | bytes 18874372
  107.6 48.9 %copy-start.1 = (bf16[2048,544]{0,1:T(8,128)(2,1)S(1)}, bf16[2048,544]{0,1:T(8,128)(2,1)}, u32[]{:S(2)}) copy-start(bf16[2048,544]{0,1:T(8,128)(2,1)} %param.23) | copy-start | bytes 6684676

commit v3 on v2

--- a/solution.py
+++ b/solution.py
@@ -87,7 +87,12 @@
     return dt[:, :share].reshape(rows, dt_rank), coef.reshape(rows, columns - dt_rank)
 
 
-def scatter_kernel(base_ref, spot_ref, back_ref, out_ref, x_ref, r0, r1, r2, a1, a2, send_sem, recv_sem):
+CHUNKS = 2
+
+
+def scatter_kernel(base_ref, spot_ref, back_ref, out_ref, *scratch):
+    held = (scratch[0:6], scratch[6:12])
+    send_sem, recv_sem = scratch[12:]
     me = lax.axis_index("tensor")
     y, z = lax.rem(me, 2), me // 2
     h = z // 2
@@ -105,29 +110,31 @@
     for d in range(3):
         pl.semaphore_signal(barrier, inc=1, device_id={"tensor": place(flipped(d))}, device_id_type=MESH)
     pl.semaphore_wait(barrier, 3)
-    width = out_ref.shape[1]
-    half = width // 2
-    orders = ((0, 1, 2), (1, 2, 0))
-
-    def send(flow, n, src, dst, d):
+    rows, width = out_ref.shape
+    lines = rows // CHUNKS
+    starts, sizes = (0, 3 * width // 4), (3 * width // 4, width // 4)
+    orders = ((0, 1, 2), (1, 0, 2))
+    units = [(chunk, flow) for chunk in range(CHUNKS) for flow in range(2)]
+
+    def send(unit, n, src, dst, d):
+        at = (unit[0] * 2 + unit[1]) * 7 + n
         copy = pltpu.make_async_remote_copy(
             src_ref=src,
             dst_ref=dst,
-            send_sem=send_sem.at[flow * 7 + n],
-            recv_sem=recv_sem.at[flow * 7 + n],
+            send_sem=send_sem.at[at],
+            recv_sem=recv_sem.at[at],
             device_id={"tensor": place(flipped(d))},
             device_id_type=MESH,
         )
         copy.start()
         return copy
 
-    def columns(flow, sel):
-        return pl.ds(pl.multiple_of(place(sel) * width + flow * half, 128), half)
-
-    def block(flow, sel):
-        where = columns(flow, sel)
-        extra = jnp.dot(spot_ref[...], back_ref[:, where], preferred_element_type=jnp.float32)
-        return base_ref[:, where] + extra
+    def block(unit, sel):
+        chunk, flow = unit
+        part = pl.ds(chunk * lines, lines)
+        where = pl.ds(pl.multiple_of(place(sel) * width + starts[flow], 128), sizes[flow])
+        extra = jnp.dot(spot_ref[part, :], back_ref[:, where], preferred_element_type=jnp.float32)
+        return base_ref[part, where] + extra
 
     def chosen(order, values):
         sel = [None] * 3
@@ -135,69 +142,78 @@
             sel[d] = v
         return tuple(sel)
 
-    first, second, third = [[], []], [[], []], [None, None]
-    for p in range(2):
-        for q in range(2):
-            for flow in range(2):
-                o = orders[flow]
-                b1 = 1 - bits[o[1]] if p == 0 else bits[o[1]]
+    first = {unit: [] for unit in units}
+    second = {unit: [] for unit in units}
+    third = {}
+    for unit in units:
+        chunk, flow = unit
+        x_ref, r0 = held[flow][0], held[flow][1]
+        o = orders[flow]
+        for p in range(2):
+            b1 = 1 - bits[o[1]] if p == 0 else bits[o[1]]
+            for q in range(2):
+                n = p * 2 + q
                 sel = chosen(o, (1 - bits[o[0]], b1, q))
-                n = p * 2 + q
-                x_ref[flow, n] = block(flow, sel).astype(jnp.bfloat16)
-                first[flow].append(send(flow, n, x_ref.at[flow, n], r0.at[flow, n], o[0]))
-    for q in range(2):
-        for flow in range(2):
-            o = orders[flow]
-            first[flow][q].wait_recv()
-            sel = chosen(o, (bits[o[0]], 1 - bits[o[1]], q))
-            own = block(flow, sel)
-            a1[flow, q] = (own + r0[flow, q].astype(jnp.float32)).astype(jnp.bfloat16)
-            second[flow].append(send(flow, 4 + q, a1.at[flow, q], r1.at[flow, q], o[1]))
-    for q in range(2):
-        for flow in range(2):
-            o = orders[flow]
-            first[flow][2 + q].wait_recv()
-            sel = chosen(o, (bits[o[0]], bits[o[1]], q))
-            own = block(flow, sel)
-            a2[flow, q] = own + r0[flow, 2 + q].astype(jnp.float32)
-    for flow in range(2):
+                x_ref[chunk, n] = block(unit, sel).astype(jnp.bfloat16)
+                first[unit].append(send(unit, n, x_ref.at[chunk, n], r0.at[chunk, n], o[0]))
+    for unit in units:
+        chunk, flow = unit
+        x_ref, r0, r1, r2, a1, a2 = held[flow]
         o = orders[flow]
         for q in range(2):
-            second[flow][q].wait_recv()
-        want = 1 - bits[o[2]]
-        a1[flow, 2] = (a2[flow, want] + r1[flow, want].astype(jnp.float32)).astype(jnp.bfloat16)
-        third[flow] = send(flow, 6, a1.at[flow, 2], r2.at[flow], o[2])
-    for flow in range(2):
-        o = orders[flow]
-        keep = bits[o[2]]
-        third[flow].wait_recv()
-        out_ref[:, flow * half : (flow + 1) * half] = (
-            a2[flow, keep] + r1[flow, keep].astype(jnp.float32) + r2[flow].astype(jnp.float32)
+            sel = chosen(o, (bits[o[0]], 1 - bits[o[1]], q))
+            own = block(unit, sel)
+            first[unit][q].wait_recv()
+            a1[chunk, q] = (own + r0[chunk, q].astype(jnp.float32)).astype(jnp.bfloat16)
+            second[unit].append(send(unit, 4 + q, a1.at[chunk, q], r1.at[chunk, q], o[1]))
+        for q in range(2):
+            sel = chosen(o, (bits[o[0]], bits[o[1]], q))
+            own = block(unit, sel)
+            first[unit][2 + q].wait_recv()
+            a2[chunk, q] = own + r0[chunk, 2 + q].astype(jnp.float32)
+    for unit in units:
+        chunk, flow = unit
+        x_ref, r0, r1, r2, a1, a2 = held[flow]
+        for q in range(2):
+            second[unit][q].wait_recv()
+        want = 1 - bits[2]
+        a1[chunk, 2] = (a2[chunk, want] + r1[chunk, want].astype(jnp.float32)).astype(jnp.bfloat16)
+        third[unit] = send(unit, 6, a1.at[chunk, 2], r2.at[chunk], 2)
+    for unit in units:
+        chunk, flow = unit
+        x_ref, r0, r1, r2, a1, a2 = held[flow]
+        keep = bits[2]
+        third[unit].wait_recv()
+        out_ref[chunk * lines : (chunk + 1) * lines, starts[flow] : starts[flow] + sizes[flow]] = (
+            a2[chunk, keep] + r1[chunk, keep].astype(jnp.float32) + r2[chunk].astype(jnp.float32)
         ).astype(jnp.bfloat16)
-    for flow in range(2):
-        for copy in first[flow] + second[flow] + [third[flow]]:
+    for unit in units:
+        for copy in first[unit] + second[unit] + [third[unit]]:
             copy.wait_send()
 
 
 def scattered(base, spot, back, parts):
     rows, width = base.shape
     own = width // parts
-    half = own // 2
+    lines = rows // CHUNKS
+    buffers = []
+    for size in (3 * own // 4, own // 4):
+        for shape, dtype in (
+            ((CHUNKS, 4, lines, size), jnp.bfloat16),
+            ((CHUNKS, 4, lines, size), jnp.bfloat16),
+            ((CHUNKS, 2, lines, size), jnp.bfloat16),
+            ((CHUNKS, lines, size), jnp.bfloat16),
+            ((CHUNKS, 3, lines, size), jnp.bfloat16),
+            ((CHUNKS, 2, lines, size), jnp.float32),
+        ):
+            buffers.append(pltpu.VMEM(shape, dtype))
+    dma = pltpu.SemaphoreType.DMA((14 * CHUNKS,))
     return pl.pallas_call(
         scatter_kernel,
         out_shape=jax.ShapeDtypeStruct((rows, own), jnp.bfloat16),
         in_specs=[pl.BlockSpec(memory_space=pltpu.VMEM)] * 3,
         out_specs=pl.BlockSpec(memory_space=pltpu.VMEM),
-        scratch_shapes=[
-            pltpu.VMEM((2, 4, rows, half), jnp.bfloat16),
-            pltpu.VMEM((2, 4, rows, half), jnp.bfloat16),
-            pltpu.VMEM((2, 2, rows, half), jnp.bfloat16),
-            pltpu.VMEM((2, rows, half), jnp.bfloat16),
-            pltpu.VMEM((2, 3, rows, half), jnp.bfloat16),
-            pltpu.VMEM((2, 2, rows, half), jnp.float32),
-            pltpu.SemaphoreType.DMA((14,)),
-            pltpu.SemaphoreType.DMA((14,)),
-        ],
+        scratch_shapes=buffers + [dma, dma],
         compiler_params=pltpu.CompilerParams(
             collective_id=1, has_side_effects=True, vmem_limit_bytes=32 << 20
         ),

time: 157 us -> 159 us (1.013)
  no operation moved by 1% of the time
where the time goes in v3:
time: 159 us; the launch traced here: 158 us
  Pallas kernels  112 us (70%)
  other arithmetic  18.8 us (12%)
  local copies, waits for them, and re-layouts  12.9 us (8%)
  matrix products  6.86 us (4%)
  starting transfers between devices  4.92 us (3%)
    pallas_call x1, Pallas kernels, scattered(): pl.pallas_call(scatter_kernel, out_shape=jax.ShapeDtypeStruct((rows, own)...  49.6 us
    pallas_call x1, Pallas kernels, dispatched(): pl.pallas_call(functools.partial(dispatch_kernel, n_dp, parts), out_shape...  40.4 us
    pallas_call x1, Pallas kernels, summed_and_normed(): pl.pallas_call(functools.partial(norm_kernel, parts, dt_rank), out_shape=...  22.5 us
    reduce_sum x1, other arithmetic, body(): jnp.sum(state * out_coef[:, :, None], axis=1) + channel_skip_gain * conv_out  15.2 us
    unnamed x34, local copies, waits for them, and re-layouts  9.75 us
    all_to_all x1, starting transfers between devices, adapted(): back = lax.all_to_all(delta, 'dp', split_axis=0, concat_axis=0, tiled=True)  4.18 us
    dot_general x3, matrix products, body(): jnp.dot(dt_low, step_size_projection, preferred_element_type=jnp.float32)  3.81 us
  transfers between devices with their start and end apart: 2, of which 1 were waited for; matrix products, arithmetic and copies ran while one was open for 17% of the time, Pallas kernels for 14%

profile of v3, /device:TPU:9, one launch (start us, length us, event | category | flops | bytes accessed | tf_op | source)
XLA Modules:
  0.0 158.0 jit_solution(3996798726457436424)
XLA Ops:
  0.7 0.7 collective-permute-start
  1.4 1.2 constant_dynamic-update-slice_fusion.1
  2.6 1.2 constant_dynamic-update-slice_fusion
  3.8 0.5 multiply_reduce_fusion.5
  4.4 0.1 copy-done.13
  4.5 1.2 fusion.31
  5.7 1.0 fusion
  6.8 22.5 %shard_map.167 = (bf16[8,32,512]{2,1,0:T(8,128)(2,1)S(1)}, f32[8,24,32]{2,1,0:T(8,128)S(1)}) custom-call(f32[8,24,544]{2,1,0:T(8,128)S(1)} %bitcast.46, f32[1,512]{1,0:T(1,128)S(1)} %bitcast.49), custom_call_target="tpu_custom_call" | custom-call | tf_op jit(solution)/shard_map/pallas_call | solution.py:71
  29.3 0.7 fusion.35
  30.0 1.5 fusion.36
  31.5 1.7 %fusion.37 = (f32[64,2048]{1,0:T(8,128)}, f32[64,2048]{1,0:T(8,128)}) fusion(f32[2048]{0:T(1024)S(1)} %copy-done.11, bf16[512,2048]{1,0:T(8,128)(2,1)S(1)} %copy-done.6, bf16[192,512]{1,0:T(8,128)(2,1)S(1)} %bitcast.55), kind=kOutput, calls=%fused_computation.104 | convolution fusion | flops 135266304 | bytes 3219456 | tf_op jit(solution)/shard_map/dot_general | solution.py:425
  33.2 0.6 fusion.34
  33.9 15.2 %multiply_reduce_fusion.2 = (f32[64,2048]{1,0:T(8,128)S(1)}, f32[64,2048]{1,0:T(8,128)S(1)}, f32[64,2048]{1,0:T(8,128)S(1)}, f32[64,16,2048]{2,1,0:T(8,128)}) fusion(f32[64,16,2048]{2,1,0:T(8,128)} %param.19, f32[64,16]{1,0:T(8,128)S(1)} %get-tuple-element.38, f32[64,2048]{1,0:T(8,128)S(1)} %get-tuple-element.24, f32[64,16]{1,0:T(8,128)} %get-tuple-element.39, ...), kind=kLoop, calls=%fused_computation.5 | loop fusion | flops 43646976 | bytes 23224320 | tf_op jit(solution)/shard_map/reduce_sum | solution.py:430
  49.0 0.5 fusion.20
  49.9 0.2 convert_reduce_fusion
  50.2 0.3 broadcast_and_fusion
  50.4 0.3 and.66
  50.7 0.4 convolution_convert_fusion.2
  51.1 0.4 convolution_convert_fusion.1
  51.5 0.2 convert_reduce_fusion.1
  51.7 0.2 select_reduce_fusion.1
  52.4 0.2 pad_maximum_fusion.outgoing_ref
  52.6 2.2 %copy-done.4 = bf16[2,16384,64]{1,2,0:T(8,128)(2,1)S(1)} copy-done((bf16[2,16384,64]{1,2,0:T(8,128)(2,1)S(1)}, bf16[2,16384,64]{1,2,0:T(8,128)(2,1)}, u32[]{:S(2)}) %copy-start.4) | copy-done | bytes 4194328
  54.8 40.4 %shard_map.168 = (f32[192,8192]{1,0:T(8,128)S(1)}, f32[2,24,128]{2,1,0:T(8,128)S(1)}) custom-call(bf16[192,2048]{1,0:T(8,128)(2,1)S(1)} %pad_maximum_fusion.1.x_ref, bf16[16,48,1024]{2,1,0:T(8,128)(2,1)S(1)} %pad_maximum_fusion.outgoing_ref, bf16[128,16384]{1,0:T(8,128)(2,1)S(1)} %bitcast.43, bf16[2048,8192]{1,0:T(8,128)(2,1)} %w_ref.1), custom_call_target="tpu_custom_call" | custom-call | tf_op jit(solution)/shard_map/pallas_call | solution.py:288
  95.1 2.6 %copy-done.2 = f32[192,8192]{1,0:T(8,128)} copy-done((f32[192,8192]{1,0:T(8,128)}, f32[192,8192]{1,0:T(8,128)S(1)}, u32[]{:S(2)}) %copy-start.2) | copy-done | bytes 6291480
  97.8 1.3 convolution_convert_fusion
  99.1 4.2 %all-to-all-start = ((bf16[2,24,8192]{2,1,0:T(8,128)(2,1)}), bf16[2,24,8192]{2,1,0:T(8,128)(2,1)S(1)}, u32[]{:S(2)}, u32[]{:S(2)}) async-start(bf16[2,24,8192]{2,1,0:T(8,128)(2,1)} %bitcast.22), calls=%async_computation | async-start | bytes 1572864 | tf_op jit(solution)/shard_map/all_to_all | solution.py:357
  103.4 0.3 and.67
  103.8 1.1 all-to-all-done
  104.9 2.8 %copy-done.3 = f32[192,8192]{1,0:T(8,128)S(1)} copy-done((f32[192,8192]{1,0:T(8,128)S(1)}, f32[192,8192]{1,0:T(8,128)}, u32[]{:S(2)}) %copy-start.3) | copy-done | bytes 6291480
  107.7 49.6 %shard_map.169 = bf16[192,1024]{1,0:T(8,128)(2,1)S(1)} custom-call(f32[192,8192]{1,0:T(8,128)S(1)} %copy-done.3, bf16[192,48]{1,0:T(8,128)(2,1)S(1)} %bitcast.48, bf16[48,8192]{1,0:T(8,128)(2,1)S(1)} %bitcast.44), custom_call_target="tpu_custom_call" | custom-call | tf_op jit(solution)/shard_map/pallas_call | solution.py:211
  157.3 0.7 copy.25
  (54 shorter events, 1.2 us)
Async XLA Ops:
  0.6 5.1 %copy-start = (bf16[2048,544]{0,1:T(8,128)(2,1)S(1)}, bf16[2048,544]{0,1:T(8,128)(2,1)}, u32[]{:S(2)}) copy-start(bf16[2048,544]{0,1:T(8,128)(2,1)} %param.23) | copy-start | bytes 6684676
  0.6 3.1 %copy-start.12 = (f32[4,2048]{1,0:T(4,128)S(1)}, f32[4,2048]{1,0:T(4,128)}, u32[]{:S(2)}) copy-start(f32[4,2048]{1,0:T(4,128)} %param.21) | copy-start | bytes 98308
  0.7 49.2 %collective-permute-start = (s32[64]{0:T(128)}, s32[64]{0:T(128)S(1)}, u32[]{:S(2)}, u32[]{:S(2)}) collective-permute-start(s32[64]{0:T(128)} %param.20), channel_id=1, source_target_pairs={{0,8},{8,0},{1,9},{9,1},{2,10},{10,2},{3,11},{11,3},{4,12},{12,4},... | collective-permute-start | bytes 776 | tf_op jit(solution)/shard_map/ppermute | solution.py:434
  3.8 0.7 copy-start.13
  5.7 1.0 copy-start.5
  5.7 23.6 %copy-start.6 = (bf16[512,2048]{1,0:T(8,128)(2,1)S(1)}, bf16[512,2048]{1,0:T(8,128)(2,1)}, u32[]{:S(2)}) copy-start(bf16[512,2048]{1,0:T(8,128)(2,1)} %param.25) | copy-start | bytes 6291460
  5.7 23.6 %copy-start.11 = (f32[2048]{0:T(1024)S(1)}, f32[2048]{0:T(1024)}, u32[]{:S(2)}) copy-start(f32[2048]{0:T(1024)} %param.26) | copy-start | bytes 24580
  31.5 2.4 %copy-start.7 = (f32[64,2048]{1,0:T(8,128)S(1)}, f32[64,2048]{1,0:T(8,128)}, u32[]{:S(2)}) copy-start(f32[64,2048]{1,0:T(8,128)} %get-tuple-element.43) | copy-start | bytes 1572868
  31.5 2.4 %copy-start.10 = (f32[16,2048]{1,0:T(8,128)S(1)}, f32[16,2048]{1,0:T(8,128)}, u32[]{:S(2)}) copy-start(f32[16,2048]{1,0:T(8,128)} %param.27) | copy-start | bytes 393220
  33.8 15.2 %copy-start.9 = (bf16[64,3,2048]{2,0,1:T(8,128)(2,1)S(1)}, bf16[64,3,2048]{2,0,1:T(8,128)(2,1)}, u32[]{:S(2)}) copy-start(bf16[64,3,2048]{2,0,1:T(8,128)(2,1)} %param.17) | copy-start | bytes 2359300
  33.8 15.2 %copy-start.14 = (f32[2048]{0:T(1024)S(1)}, f32[2048]{0:T(1024)}, u32[]{:S(2)}) copy-start(f32[2048]{0:T(1024)} %param.28) | copy-start | bytes 24580
  49.0 0.8 copy-start.15
  52.6 2.2 %copy-start.4 = (bf16[2,16384,64]{1,2,0:T(8,128)(2,1)S(1)}, bf16[2,16384,64]{1,2,0:T(8,128)(2,1)}, u32[]{:S(2)}) copy-start(bf16[2,16384,64]{1,2,0:T(8,128)(2,1)} %param.30) | copy-start | bytes 12582916
  54.8 43.1 %copy-start.8 = (bf16[2,64,8192]{2,1,0:T(8,128)(2,1)S(1)}, bf16[2,64,8192]{2,1,0:T(8,128)(2,1)}, u32[]{:S(2)}) copy-start(bf16[2,64,8192]{2,1,0:T(8,128)(2,1)} %param.31) | copy-start | bytes 6291460
  95.1 2.7 %copy-start.2 = (f32[192,8192]{1,0:T(8,128)}, f32[192,8192]{1,0:T(8,128)S(1)}, u32[]{:S(2)}) copy-start(f32[192,8192]{1,0:T(8,128)S(1)} %get-tuple-element.8.base_ref) | copy-start | bytes 18874372
  99.1 5.8 %all-to-all-start = ((bf16[2,24,8192]{2,1,0:T(8,128)(2,1)}), bf16[2,24,8192]{2,1,0:T(8,128)(2,1)S(1)}, u32[]{:S(2)}, u32[]{:S(2)}) async-start(bf16[2,24,8192]{2,1,0:T(8,128)(2,1)} %bitcast.22), calls=%async_computation | async-start | bytes 1572864 | tf_op jit(solution)/shard_map/all_to_all | solution.py:357
  104.9 2.8 %copy-start.3 = (f32[192,8192]{1,0:T(8,128)S(1)}, f32[192,8192]{1,0:T(8,128)}, u32[]{:S(2)}) copy-start(f32[192,8192]{1,0:T(8,128)} %copy-done.2) | copy-start | bytes 18874372
  107.7 50.3 %copy-start.1 = (bf16[2048,544]{0,1:T(8,128)(2,1)S(1)}, bf16[2048,544]{0,1:T(8,128)(2,1)}, u32[]{:S(2)}) copy-start(bf16[2048,544]{0,1:T(8,128)(2,1)} %param.23) | copy-start | bytes 6684676

commit v4 on v3

--- a/solution.py
+++ b/solution.py
@@ -220,8 +220,10 @@
     )(base, spot, back)
 
 
-def dispatch_kernel(n_dp, parts, x_ref, outgoing_ref, down_ref, w_ref, base_ref, coef_ref, held, total, send_sem, recv_sem):
+def dispatch_kernel(n_dp, parts, x_ref, outgoing_ref, down_ref, w_ref, base_ref, coef_ref, held, total, down_here, down_sem, send_sem, recv_sem):
     owners = n_dp * parts
+    fetch = pltpu.make_async_copy(down_ref, down_here, down_sem)
+    fetch.start()
     me = lax.axis_index("dp") * parts + lax.axis_index("tensor")
 
     def device(peer):
@@ -260,6 +262,7 @@
     half = depth // 2
     lines = held.shape[1] // 2
     total[...] = jnp.zeros_like(total)
+    fetch.wait()
     for k in range(owners):
         source = lax.rem(me - k + owners, owners)
         part = lax.rem(source, parts)
@@ -273,7 +276,7 @@
             where = pl.ds(pl.multiple_of(part * depth + side * half, 128), half)
             found.append(
                 lax.dot_general(
-                    rows_in, down_ref[:, where], (((1,), (1,)), ((), ())), preferred_element_type=jnp.float32
+                    rows_in, down_here[:, where], (((1,), (1,)), ((), ())), preferred_element_type=jnp.float32
                 )
             )
         total[source // parts] += found[0][:lines] + found[1][lines:]
@@ -291,11 +294,13 @@
             jax.ShapeDtypeStruct((x.shape[0], w.shape[1]), jnp.float32),
             jax.ShapeDtypeStruct((n_dp, lines // 2, down.shape[0]), jnp.float32),
         ),
-        in_specs=[pl.BlockSpec(memory_space=pltpu.VMEM)] * 3 + [pl.BlockSpec(memory_space=pl.ANY)],
+        in_specs=[pl.BlockSpec(memory_space=pltpu.VMEM)] * 2 + [pl.BlockSpec(memory_space=pl.ANY)] * 2,
         out_specs=(pl.BlockSpec(memory_space=pl.ANY), pl.BlockSpec(memory_space=pltpu.VMEM)),
         scratch_shapes=[
             pltpu.VMEM((owners - 1, lines, half), jnp.bfloat16),
             pltpu.VMEM((n_dp, lines // 2, down.shape[0]), jnp.float32),
+            pltpu.VMEM(down.shape, jnp.bfloat16),
+            pltpu.SemaphoreType.DMA,
             dma,
             dma,
         ],

time: 159 us -> 159 us (level)
  no operation moved by 1% of the time
where the time goes in v4:
time: 159 us; the launch traced here: 158 us
  Pallas kernels  113 us (71%)
  other arithmetic  18.8 us (12%)
  local copies, waits for them, and re-layouts  12.9 us (8%)
  matrix products  6.86 us (4%)
  starting transfers between devices  4.93 us (3%)
    pallas_call x1, Pallas kernels, scattered(): pl.pallas_call(scatter_kernel, out_shape=jax.ShapeDtypeStruct((rows, own)...  49.3 us
    pallas_call x1, Pallas kernels, dispatched(): pl.pallas_call(functools.partial(dispatch_kernel, n_dp, parts), out_shape...  40.8 us
    pallas_call x1, Pallas kernels, summed_and_normed(): pl.pallas_call(functools.partial(norm_kernel, parts, dt_rank), out_shape=...  22.5 us
    reduce_sum x1, other arithmetic, body(): jnp.sum(state * out_coef[:, :, None], axis=1) + channel_skip_gain * conv_out  15.2 us
    unnamed x34, local copies, waits for them, and re-layouts  9.75 us
    all_to_all x1, starting transfers between devices, adapted(): back = lax.all_to_all(delta, 'dp', split_axis=0, concat_axis=0, tiled=True)  4.19 us
    dot_general x3, matrix products, body(): jnp.dot(dt_low, step_size_projection, preferred_element_type=jnp.float32)  3.81 us
  transfers between devices with their start and end apart: 2, of which 1 were waited for; matrix products, arithmetic and copies ran while one was open for 17% of the time, Pallas kernels for 14%

profile of v4, /device:TPU:9, one launch (start us, length us, event | category | flops | bytes accessed | tf_op | source)
XLA Modules:
  0.0 158.2 jit_solution(9689580527650533914)
XLA Ops:
  0.7 0.7 collective-permute-start
  1.4 1.2 constant_dynamic-update-slice_fusion.1
  2.6 1.2 constant_dynamic-update-slice_fusion
  3.8 0.5 multiply_reduce_fusion.5
  4.4 0.1 copy-done.13
  4.5 1.2 fusion.31
  5.7 1.0 fusion
  6.8 22.5 %shard_map.167 = (bf16[8,32,512]{2,1,0:T(8,128)(2,1)S(1)}, f32[8,24,32]{2,1,0:T(8,128)S(1)}) custom-call(f32[8,24,544]{2,1,0:T(8,128)S(1)} %bitcast.46, f32[1,512]{1,0:T(1,128)S(1)} %bitcast.49), custom_call_target="tpu_custom_call" | custom-call | tf_op jit(solution)/shard_map/pallas_call | solution.py:71
  29.3 0.7 fusion.35
  30.0 1.5 fusion.36
  31.5 1.7 %fusion.37 = (f32[64,2048]{1,0:T(8,128)}, f32[64,2048]{1,0:T(8,128)}) fusion(f32[2048]{0:T(1024)S(1)} %copy-done.11, bf16[512,2048]{1,0:T(8,128)(2,1)S(1)} %copy-done.6, bf16[192,512]{1,0:T(8,128)(2,1)S(1)} %bitcast.55), kind=kOutput, calls=%fused_computation.104 | convolution fusion | flops 135266304 | bytes 3219456 | tf_op jit(solution)/shard_map/dot_general | solution.py:430
  33.2 0.6 fusion.34
  33.9 15.2 %multiply_reduce_fusion.2 = (f32[64,2048]{1,0:T(8,128)S(1)}, f32[64,2048]{1,0:T(8,128)S(1)}, f32[64,2048]{1,0:T(8,128)S(1)}, f32[64,16,2048]{2,1,0:T(8,128)}) fusion(f32[64,16,2048]{2,1,0:T(8,128)} %param.19, f32[64,16]{1,0:T(8,128)S(1)} %get-tuple-element.38, f32[64,2048]{1,0:T(8,128)S(1)} %get-tuple-element.24, f32[64,16]{1,0:T(8,128)} %get-tuple-element.39, ...), kind=kLoop, calls=%fused_computation.5 | loop fusion | flops 43646976 | bytes 23224320 | tf_op jit(solution)/shard_map/reduce_sum | solution.py:435
  49.0 0.5 fusion.20
  49.9 0.2 convert_reduce_fusion
  50.2 0.3 broadcast_and_fusion
  50.4 0.3 and.66
  50.7 0.4 convolution_convert_fusion.2
  51.1 0.4 convolution_convert_fusion.1
  51.5 0.2 convert_reduce_fusion.1
  51.7 0.2 select_reduce_fusion.1
  52.4 0.2 pad_maximum_fusion.outgoing_ref
  52.6 2.2 %copy-done.4 = bf16[2,16384,64]{1,2,0:T(8,128)(2,1)S(1)} copy-done((bf16[2,16384,64]{1,2,0:T(8,128)(2,1)S(1)}, bf16[2,16384,64]{1,2,0:T(8,128)(2,1)}, u32[]{:S(2)}) %copy-start.4) | copy-done | bytes 4194328
  54.8 40.8 %shard_map.168 = (f32[192,8192]{1,0:T(8,128)S(1)}, f32[2,24,128]{2,1,0:T(8,128)S(1)}) custom-call(bf16[192,2048]{1,0:T(8,128)(2,1)S(1)} %pad_maximum_fusion.1.x_ref, bf16[16,48,1024]{2,1,0:T(8,128)(2,1)S(1)} %pad_maximum_fusion.outgoing_ref, bf16[128,16384]{1,0:T(8,128)(2,1)S(1)} %bitcast.43, bf16[2048,8192]{1,0:T(8,128)(2,1)} %w_ref.1), custom_call_target="tpu_custom_call" | custom-call | tf_op jit(solution)/shard_map/pallas_call | solution.py:291
  95.6 2.6 %copy-done.2 = f32[192,8192]{1,0:T(8,128)} copy-done((f32[192,8192]{1,0:T(8,128)}, f32[192,8192]{1,0:T(8,128)S(1)}, u32[]{:S(2)}) %copy-start.2) | copy-done | bytes 6291480
  98.2 1.3 convolution_convert_fusion
  99.5 4.2 %all-to-all-start = ((bf16[2,24,8192]{2,1,0:T(8,128)(2,1)}), bf16[2,24,8192]{2,1,0:T(8,128)(2,1)S(1)}, u32[]{:S(2)}, u32[]{:S(2)}) async-start(bf16[2,24,8192]{2,1,0:T(8,128)(2,1)} %bitcast.22), calls=%async_computation | async-start | bytes 1572864 | tf_op jit(solution)/shard_map/all_to_all | solution.py:362
  103.8 0.3 and.67
  104.2 1.1 all-to-all-done
  105.3 2.8 %copy-done.3 = f32[192,8192]{1,0:T(8,128)S(1)} copy-done((f32[192,8192]{1,0:T(8,128)S(1)}, f32[192,8192]{1,0:T(8,128)}, u32[]{:S(2)}) %copy-start.3) | copy-done | bytes 6291480
  108.1 49.3 %shard_map.169 = bf16[192,1024]{1,0:T(8,128)(2,1)S(1)} custom-call(f32[192,8192]{1,0:T(8,128)S(1)} %copy-done.3, bf16[192,48]{1,0:T(8,128)(2,1)S(1)} %bitcast.48, bf16[48,8192]{1,0:T(8,128)(2,1)S(1)} %bitcast.44), custom_call_target="tpu_custom_call" | custom-call | tf_op jit(solution)/shard_map/pallas_call | solution.py:211
  157.4 0.7 copy.25
  (54 shorter events, 1.2 us)
Async XLA Ops:
  0.6 5.1 %copy-start = (bf16[2048,544]{0,1:T(8,128)(2,1)S(1)}, bf16[2048,544]{0,1:T(8,128)(2,1)}, u32[]{:S(2)}) copy-start(bf16[2048,544]{0,1:T(8,128)(2,1)} %param.23) | copy-start | bytes 6684676
  0.6 3.1 %copy-start.12 = (f32[4,2048]{1,0:T(4,128)S(1)}, f32[4,2048]{1,0:T(4,128)}, u32[]{:S(2)}) copy-start(f32[4,2048]{1,0:T(4,128)} %param.21) | copy-start | bytes 98308
  0.7 49.2 %collective-permute-start = (s32[64]{0:T(128)}, s32[64]{0:T(128)S(1)}, u32[]{:S(2)}, u32[]{:S(2)}) collective-permute-start(s32[64]{0:T(128)} %param.20), channel_id=1, source_target_pairs={{0,8},{8,0},{1,9},{9,1},{2,10},{10,2},{3,11},{11,3},{4,12},{12,4},... | collective-permute-start | bytes 776 | tf_op jit(solution)/shard_map/ppermute | solution.py:439
  3.8 0.7 copy-start.13
  5.7 1.0 copy-start.5
  5.7 23.6 %copy-start.6 = (bf16[512,2048]{1,0:T(8,128)(2,1)S(1)}, bf16[512,2048]{1,0:T(8,128)(2,1)}, u32[]{:S(2)}) copy-start(bf16[512,2048]{1,0:T(8,128)(2,1)} %param.25) | copy-start | bytes 6291460
  5.7 23.6 %copy-start.11 = (f32[2048]{0:T(1024)S(1)}, f32[2048]{0:T(1024)}, u32[]{:S(2)}) copy-start(f32[2048]{0:T(1024)} %param.26) | copy-start | bytes 24580
  31.5 2.4 %copy-start.7 = (f32[64,2048]{1,0:T(8,128)S(1)}, f32[64,2048]{1,0:T(8,128)}, u32[]{:S(2)}) copy-start(f32[64,2048]{1,0:T(8,128)} %get-tuple-element.43) | copy-start | bytes 1572868
  31.5 2.4 %copy-start.10 = (f32[16,2048]{1,0:T(8,128)S(1)}, f32[16,2048]{1,0:T(8,128)}, u32[]{:S(2)}) copy-start(f32[16,2048]{1,0:T(8,128)} %param.27) | copy-start | bytes 393220
  33.8 15.2 %copy-start.9 = (bf16[64,3,2048]{2,0,1:T(8,128)(2,1)S(1)}, bf16[64,3,2048]{2,0,1:T(8,128)(2,1)}, u32[]{:S(2)}) copy-start(bf16[64,3,2048]{2,0,1:T(8,128)(2,1)} %param.17) | copy-start | bytes 2359300
  33.8 15.2 %copy-start.14 = (f32[2048]{0:T(1024)S(1)}, f32[2048]{0:T(1024)}, u32[]{:S(2)}) copy-start(f32[2048]{0:T(1024)} %param.28) | copy-start | bytes 24580
  49.0 0.8 copy-start.15
  52.6 2.2 %copy-start.4 = (bf16[2,16384,64]{1,2,0:T(8,128)(2,1)S(1)}, bf16[2,16384,64]{1,2,0:T(8,128)(2,1)}, u32[]{:S(2)}) copy-start(bf16[2,16384,64]{1,2,0:T(8,128)(2,1)} %param.30) | copy-start | bytes 12582916
  54.8 43.5 %copy-start.8 = (bf16[2,64,8192]{2,1,0:T(8,128)(2,1)S(1)}, bf16[2,64,8192]{2,1,0:T(8,128)(2,1)}, u32[]{:S(2)}) copy-start(bf16[2,64,8192]{2,1,0:T(8,128)(2,1)} %param.31) | copy-start | bytes 6291460
  95.5 2.7 %copy-start.2 = (f32[192,8192]{1,0:T(8,128)}, f32[192,8192]{1,0:T(8,128)S(1)}, u32[]{:S(2)}) copy-start(f32[192,8192]{1,0:T(8,128)S(1)} %get-tuple-element.8.base_ref) | copy-start | bytes 18874372
  99.5 5.8 %all-to-all-start = ((bf16[2,24,8192]{2,1,0:T(8,128)(2,1)}), bf16[2,24,8192]{2,1,0:T(8,128)(2,1)S(1)}, u32[]{:S(2)}, u32[]{:S(2)}) async-start(bf16[2,24,8192]{2,1,0:T(8,128)(2,1)} %bitcast.22), calls=%async_computation | async-start | bytes 1572864 | tf_op jit(solution)/shard_map/all_to_all | solution.py:362
  105.3 2.8 %copy-start.3 = (f32[192,8192]{1,0:T(8,128)S(1)}, f32[192,8192]{1,0:T(8,128)}, u32[]{:S(2)}) copy-start(f32[192,8192]{1,0:T(8,128)} %copy-done.2) | copy-start | bytes 18874372
  108.1 50.0 %copy-start.1 = (bf16[2048,544]{0,1:T(8,128)(2,1)S(1)}, bf16[2048,544]{0,1:T(8,128)(2,1)}, u32[]{:S(2)}) copy-start(bf16[2048,544]{0,1:T(8,128)(2,1)} %param.23) | copy-start | bytes 6684676
